TPU v7x, 512 devices: a whole 4x8x8 slice. The times are simulated.
512 devices in a mesh: planes: 64 (over z, y_hi, core), lines: 8 (over y_lo, x).
Axes of the slice: x: 4, y: 8 (y_hi: 4, y_lo: 2; y = y_hi * 2 + y_lo), z: 8, core: 2. Of those that a mesh axis runs over, the one named last changes fastest.
Arguments:
- conserved: float32 [5, 64, 256, 1024], P(None, 'planes', 'lines'), may hold values from -2 to 400, as said below
- step_ratio: float32 [], replicated, may hold values from 0.005 to 0.01
Outputs:
- advanced: float32 [5, 64, 256, 1024], P(None, 'planes', 'lines')
- step_margin: float32 [], replicated
Inputs may be any that keep to these rules, and one draw needn't show every extreme that they name: `conserved`: density lies in 0.5 to 1.5 and the pressure 0.4 (E - |m|^2 / (2 density)) is 1 or more in every cell.
All inputs are finite; a program needn't handle non-finite values.
Results may differ from a plain program's by a relative error of at most 0.0003.
Values sent between devices are 32-bit elements; how exact they have to be, the bound alone decides.
No kernel may reach another device: no remote copies, remote signals or barrier semaphores. Data moves between devices by JAX's collectives and lax.ppermute only.
A program may use at most 64 MiB of HBM per device.

v0:
```python
import functools

import jax
import jax.numpy as jnp
from jax import lax
from jax.sharding import PartitionSpec as P

adiabatic = 1.4
safety = 0.8
ghosts = 3


def window(source_array, first_cell, cell_count, along_axis):
    return lax.slice_in_dim(source_array, first_cell, first_cell + cell_count, axis=along_axis)


def primitive(fields):
    density = fields[0]
    velocity = [fields[1] / density, fields[2] / density, fields[3] / density]
    kinetic = velocity[0] * velocity[0] + velocity[1] * velocity[1] + velocity[2] * velocity[2]
    pressure = (adiabatic - 1.0) * (fields[4] - 0.5 * density * kinetic)
    return [density] + velocity + [pressure]


def face_values(values, length, along_axis):
    edge_values = 7.0 / 12.0 * (
        window(values, 1, length + 3, along_axis) + window(values, 2, length + 3, along_axis)
    ) - 1.0 / 12.0 * (
        window(values, 0, length + 3, along_axis) + window(values, 3, length + 3, along_axis)
    )
    edge_low = jnp.minimum(
        window(values, 1, length + 3, along_axis), window(values, 2, length + 3, along_axis)
    )
    edge_high = jnp.maximum(
        window(values, 1, length + 3, along_axis), window(values, 2, length + 3, along_axis)
    )
    edge_values = jnp.clip(edge_values, edge_low, edge_high)
    center = window(values, 2, length + 2, along_axis)
    to_left = window(edge_values, 0, length + 2, along_axis) - center
    to_right = window(edge_values, 1, length + 2, along_axis) - center
    monotone = to_left * to_right < 0.0
    bound_left = 2.0 * jnp.abs(to_right)
    bound_right = 2.0 * jnp.abs(to_left)
    left_face = center + jnp.where(monotone, jnp.clip(to_left, -bound_left, bound_left), 0.0)
    right_face = center + jnp.where(monotone, jnp.clip(to_right, -bound_right, bound_right), 0.0)
    return (
        window(right_face, 0, length + 1, along_axis),
        window(left_face, 1, length + 1, along_axis),
    )


def conserved_flux(primitives, normal):
    density, speed_x, speed_y, speed_z, pressure = primitives
    velocity = [speed_x, speed_y, speed_z]
    normal_speed = velocity[normal]
    energy = pressure / (adiabatic - 1.0) + 0.5 * density * (
        speed_x * speed_x + speed_y * speed_y + speed_z * speed_z
    )
    state_vector = [density, density * speed_x, density * speed_y, density * speed_z, energy]
    flux_vector = [
        density * normal_speed,
        density * speed_x * normal_speed,
        density * speed_y * normal_speed,
        density * speed_z * normal_speed,
        (energy + pressure) * normal_speed,
    ]
    flux_vector[1 + normal] = flux_vector[1 + normal] + pressure
    sound_speed = jnp.sqrt(adiabatic * pressure / density)
    return (state_vector, flux_vector, normal_speed, sound_speed)


def hll_flux(left_values, right_values, normal):
    left_state, left_flux, left_speed, left_sound = conserved_flux(left_values, normal)
    right_state, right_flux, right_speed, right_sound = conserved_flux(right_values, normal)
    slowest = jnp.minimum(jnp.minimum(left_speed - left_sound, right_speed - right_sound), 0.0)
    fastest = jnp.maximum(jnp.maximum(left_speed + left_sound, right_speed + right_sound), 0.0)
    inverse_gap = 1.0 / (fastest - slowest)
    return [
        (
            fastest * left_flux[component]
            - slowest * right_flux[component]
            + slowest * fastest * (right_state[component] - left_state[component])
        )
        * inverse_gap
        for component in range(5)
    ]


def split_sweep(padded, step_ratio, sweep_axis, normal):
    length = padded.shape[sweep_axis] - 2 * ghosts
    inner_axis = sweep_axis - 1
    primitives = primitive(padded)
    face_pairs = [face_values(quantity, length, inner_axis) for quantity in primitives]
    left_values = [entry[0] for entry in face_pairs]
    right_values = [entry[1] for entry in face_pairs]
    fluxes = hll_flux(left_values, right_values, normal)
    updated = []
    for component in range(5):
        previous = window(padded[component], ghosts, length, inner_axis)
        updated.append(
            previous
            - step_ratio
            * (
                window(fluxes[component], 1, length, inner_axis)
                - window(fluxes[component], 0, length, inner_axis)
            )
        )
    return jnp.stack(updated)


def pad_edges(fields, sweep_axis):
    widths = [(0, 0)] * fields.ndim
    widths[sweep_axis] = (ghosts, ghosts)
    return jnp.pad(fields, widths, mode="edge")


def margin_cells(fields, step_ratio):
    primitives = primitive(fields)
    sound_speed = jnp.sqrt(adiabatic * primitives[4] / primitives[0])
    signal = jnp.abs(primitives[1]) + sound_speed + (jnp.abs(primitives[2]) + sound_speed)
    return safety / (step_ratio * signal)


def body(conserved, step_ratio):
    block_count = 1
    block_size = conserved.shape[1] // block_count
    plane_block = window(conserved, 0, block_size, 1)
    x_swept = split_sweep(pad_edges(plane_block, 3), step_ratio, 3, 0)
    turned = lax.all_to_all(x_swept, "lines", split_axis=3, concat_axis=2, tiled=True)
    after_y = split_sweep(pad_edges(turned, 2), step_ratio, 2, 1)
    returned = lax.all_to_all(after_y, "lines", split_axis=2, concat_axis=3, tiled=True)
    margins = [jnp.min(margin_cells(returned, step_ratio))]
    local_margin = functools.reduce(jnp.minimum, margins)
    step_margin = lax.pmin(local_margin, ("planes", "lines"))
    return (returned, step_margin)


def solution(mesh):
    in_specs = (P(None, "planes", "lines", None), P())
    out_specs = (P(None, "planes", "lines", None), P())
    return jax.shard_map(body, mesh=mesh, in_specs=in_specs, out_specs=out_specs, check_vma=False)
```

profile of v0, /device:TPU:1, one launch (start us, length us, event | category | flops | bytes accessed | tf_op | source)
XLA Modules:
  0.0 172.7 jit_solution(10939480992590596415)
XLA Ops:
  0.6 1.0 fusion.153
  1.6 0.1 copy.52
  1.8 0.1 copy.51
  1.9 0.1 reshape.345
  2.0 0.1 reshape.346
  2.1 1.5 concatenate.8
  3.6 0.1 subtract_multiply_fusion
  3.7 0.1 slice_bitcast_fusion.2
  4.4 0.2 fusion.27
  4.5 0.3 fusion.7
  4.9 0.1 fusion.144
  5.0 0.2 multiply_compare_fusion
  5.1 0.1 fusion.145
  5.3 0.2 multiply_compare_fusion.1
  5.4 0.3 fusion.33
  5.7 0.1 fusion.146
  5.9 0.2 multiply_compare_fusion.3
  6.0 0.1 fusion.150
  6.2 0.2 multiply_compare_fusion.4
  6.3 0.1 fusion.151
  6.5 0.2 multiply_compare_fusion.2
  6.6 1.1 add_multiply_fusion
  7.8 0.4 add_multiply_fusion.1
  8.1 0.1 fusion.125
  8.3 0.1 fusion.121
  8.4 0.1 fusion.117
  8.5 0.1 fusion.113
  8.7 0.1 fusion.109
  8.8 1.9 %copy.38 = f32[5,1,32,1024]{2,1,0,3:T(1,128)S(1)} copy(f32[5,1,32,1024]{3,2,1,0:T(8,128)S(1)} %fusion.109) | data formatting | bytes 1310720 | tf_op jit(solution)/shard_map/stack | solution.py:108
  10.7 0.5 broadcast.427
  11.2 10.5 %reduce.1 = f32[1024,5,32]{2,1,0:T(8,128)} reduce(f32[1024,5,1,32]{3,2,1,0:T(1,128)S(1)} %bitcast.124, f32[]{:T(128)} %broadcast.427), dimensions={2}, to_apply=%bitcast.108.reduce_sub_computation | reduce | bytes 1310724
  21.8 3.6 %reshape.349 = f32[8,1,20480]{2,1,0:T(1,128)S(1)} reshape(f32[1024,5,32]{2,1,0:T(8,128)} %reduce.1) | data formatting | bytes 1310720
  25.3 13.9 %all_to_all.36 = f32[8,1,20480]{2,1,0:T(1,128)S(1)} all-to-all(f32[8,1,20480]{2,1,0:T(1,128)S(1)} %reshape.349), channel_id=1, replica_groups=mesh['planes'=64,'lines'=8] {'lines'}, dimensions={0} | all-to-all | bytes 1310720 | tf_op jit(solution)/shard_map/all_to_all | solution.py:129
  39.2 2.2 %reduce.2 = f32[8,20480]{1,0:T(8,128)S(1)} reduce(f32[8,1,20480]{2,1,0:T(1,128)S(1)} %all_to_all.36, f32[]{:T(128)} %broadcast.427), dimensions={1}, to_apply=%all_to_all.26.reduce_sub_computation | reduce | bytes 1310724 | tf_op jit(solution)/shard_map/all_to_all | solution.py:129
  41.4 4.4 %reshape.350 = f32[1024,5,1,32]{3,2,1,0:T(1,128)S(1)} reshape(f32[8,20480]{1,0:T(8,128)S(1)} %reduce.2) | data formatting | bytes 1310720
  45.9 3.1 %copy.39 = f32[5,1,32,1024]{3,1,2,0:T(1,128)S(1)} copy(f32[5,1,32,1024]{2,1,0,3:T(1,128)S(1)} %bitcast.125) | data formatting | bytes 1310720 | tf_op jit(solution)/shard_map/all_to_all | solution.py:129
  49.0 0.1 copy.40
  49.2 0.1 pad_maximum_fusion
  49.3 0.1 subtract_multiply_fusion.1
  49.4 0.1 fusion.73
  49.5 0.1 fusion.55
  49.6 0.1 fusion.47
  49.7 0.1 fusion.79
  49.7 0.1 fusion.67
  49.9 0.1 multiply_compare_fusion.7
  50.0 0.1 multiply_compare_fusion.9
  50.1 0.1 multiply_compare_fusion.5
  50.2 0.1 multiply_compare_fusion.6
  50.3 0.1 multiply_compare_fusion.8
  50.4 0.9 add_multiply_fusion.5
  51.3 0.3 add_multiply_fusion.6
  51.8 0.7 copy.45
  52.5 10.6 %all_to_all.37 = f32[5,1,256,128]{3,1,0,2:T(1,128)S(1)} all-to-all(f32[5,1,256,128]{3,1,0,2:T(1,128)S(1)} %copy.45), channel_id=1, replica_groups=mesh['planes'=64,'lines'=8] {'lines'}, dimensions={2} | all-to-all | bytes 1310720 | tf_op jit(solution)/shard_map/all_to_all | solution.py:131
  63.2 0.7 fusion.126
  63.9 0.4 copy.47
  64.3 107.4 %pmin.7 = f32[]{:T(128)} all-reduce(f32[]{:T(128)} %fusion.126), channel_id=1, replica_groups=mesh['planes'=64,'lines'=8] {'planes','lines'}, use_global_device_ids=true, to_apply=%region_1.2 | all-reduce | flops 1 | bytes 8 | tf_op jit(solution)/shard_map/pmin | solution.py:134
  171.7 1.0 copy.48
  (28 shorter events, 0.6 us)
where the time goes:
time: 173 us
  blocking collectives  132 us (76%)
  other arithmetic  20.3 us (12%)
  local copies, waits for them, and re-layouts  18.7 us (11%)
  between operations  1.79 us (1%)
    pmin x1, blocking collectives, body(): step_margin = lax.pmin(local_margin, ('planes', 'lines'))  107 us
    all_to_all x1, blocking collectives, body(): lax.all_to_all(x_swept, 'lines', split_axis=3, concat_axis=2, tiled=True)  13.9 us
    unnamed x9, other arithmetic  11.2 us
    all_to_all x1, blocking collectives, body(): lax.all_to_all(after_y, 'lines', split_axis=2, concat_axis=3, tiled=True)  10.6 us
    unnamed x8, local copies, waits for them, and re-layouts  9.68 us

commit v1 on v0

v1 whole, which is shorter than its diff:
```python
import functools

import jax
import jax.numpy as jnp
from jax import lax
from jax.experimental import pallas as pl
from jax.experimental.pallas import tpu as pltpu
from jax.sharding import PartitionSpec as P

adiabatic = 1.4
safety = 0.8
ghosts = 3
fields = 5
rows = 8
lanes = 128


def primitive(u):
    density, mx, my, mz, energy = u
    inverse = 1.0 / density
    vx, vy, vz = mx * inverse, my * inverse, mz * inverse
    pressure = (adiabatic - 1.0) * (energy - 0.5 * (mx * vx + my * vy + mz * vz))
    return [density, vx, vy, vz, pressure]


def edge_offset(step, step_below, step_above):
    raw = 0.5 * step + (step_below - step_above) * (1.0 / 12.0)
    return jnp.maximum(jnp.minimum(raw, jnp.maximum(step, 0.0)), jnp.minimum(step, 0.0))


def limited(offset, other):
    bound = -2.0 * other
    return jnp.maximum(jnp.minimum(offset, bound), jnp.minimum(jnp.maximum(offset, bound), 0.0))


def half_state(state, normal):
    density, pressure = state[0], state[4]
    ratio = pressure * (1.0 / density)
    sound = jnp.sqrt(adiabatic * ratio)
    kinetic = state[1] * state[1] + state[2] * state[2] + state[3] * state[3]
    specific = 1.0 / (adiabatic - 1.0) * ratio + 0.5 * kinetic
    return state[1 + normal], sound, specific


def hll_flux(left, right, normal):
    ul, cl, el = half_state(left, normal)
    ur, cr, er = half_state(right, normal)
    slowest = jnp.minimum(jnp.minimum(ul - cl, ur - cr), 0.0)
    fastest = jnp.maximum(jnp.maximum(ul + cl, ur + cr), 0.0)
    inverse = 1.0 / (fastest - slowest)
    wl, wr = fastest * inverse, slowest * inverse
    ml = left[0] * (ul - slowest) * wl
    mr = right[0] * (ur - fastest) * wr
    pl_, pr_ = left[4] * wl, right[4] * wr
    flux = [ml - mr]
    for axis in range(3):
        term = ml * left[1 + axis] - mr * right[1 + axis]
        if axis == normal:
            term = term + (pl_ - pr_)
        flux.append(term)
    flux.append((ml * el + pl_ * ul) - (mr * er + pr_ * ur))
    return flux


def own_flux(state, normal):
    density, pressure = state[0], state[4]
    speed = state[1 + normal]
    mass = density * speed
    flux = [mass] + [mass * state[1 + axis] for axis in range(3)]
    flux[1 + normal] = flux[1 + normal] + pressure
    kinetic = state[1] * state[1] + state[2] * state[2] + state[3] * state[3]
    flux.append((adiabatic / (adiabatic - 1.0) * pressure + 0.5 * density * kinetic) * speed)
    return flux


def x_sweep(u, ratio, shift_up, shift_down):
    count = len(u[0])
    q = [[], [], [], [], []]
    for t in range(count):
        for v, value in enumerate(primitive([u[f][t] for f in range(fields)])):
            q[v].append(value)
    left, right = [], []
    for v in range(fields):
        above = shift_up(q[v], q[v])
        d = [a - b for a, b in zip(above, q[v])]
        zero = [jnp.zeros_like(d[0])] * count
        dm, dp = shift_down(d, zero), shift_up(d, zero)
        a = [edge_offset(*s) for s in zip(d, dm, dp)]
        b = shift_down([i - j for i, j in zip(a, d)], zero)
        lower = [i + limited(j, k) for i, j, k in zip(q[v], b, a)]
        upper = [i + limited(k, j) for i, j, k in zip(q[v], b, a)]
        left.append(upper)
        right.append(shift_up(lower, upper))
    flux = [[], [], [], [], []]
    for t in range(count):
        got = hll_flux([s[t] for s in left], [s[t] for s in right], 0)
        for f in range(fields):
            flux[f].append(got[f])
    first = own_flux([q[v][0] for v in range(fields)], 0)
    out = []
    for f in range(fields):
        before = shift_down(flux[f], [first[f]] * count)
        out.append([i - ratio * (j - k) for i, j, k in zip(u[f], flux[f], before)])
    return out


def tile_shifts(count):
    lane = lax.broadcasted_iota(jnp.int32, (rows, lanes), 1)
    is_first, is_last = lane == 0, lane == lanes - 1

    def up(tiles, end):
        turned = [pltpu.roll(t, lanes - 1, 1) for t in tiles]
        return [
            jnp.where(is_last, turned[t + 1] if t + 1 < count else end[t], turned[t])
            for t in range(count)
        ]

    def down(tiles, end):
        turned = [pltpu.roll(t, 1, 1) for t in tiles]
        return [
            jnp.where(is_first, turned[t - 1] if t else end[t], turned[t]) for t in range(count)
        ]

    return up, down


def row_shifts():
    lane = lax.broadcasted_iota(jnp.int32, (rows, lanes), 1)
    place = lane + lanes * lax.broadcasted_iota(jnp.int32, (rows, lanes), 0)

    def up(tiles, end):
        out = []
        for t, e in zip(tiles, end):
            turned = pltpu.roll(t, lanes - 1, 1)
            turned = jnp.where(lane == lanes - 1, pltpu.roll(turned, rows - 1, 0), turned)
            out.append(jnp.where(place == rows * lanes - 1, e, turned))
        return out

    def down(tiles, end):
        out = []
        for t, e in zip(tiles, end):
            turned = pltpu.roll(t, 1, 1)
            turned = jnp.where(lane == 0, pltpu.roll(turned, 1, 0), turned)
            out.append(jnp.where(place == 0, e, turned))
        return out

    return up, down


def x_sweep_row(u, ratio, up, down):
    out = x_sweep([[value] for value in u], ratio, up, down)
    return [value[0] for value in out]


def new_march():
    return dict(q=[], d=[], a=[], upper=[], flux=[])


def march(state, u, before_update, ratio):
    q = primitive(u)
    state["q"] = state["q"][-2:] + [q]
    if len(state["q"]) < 2:
        return None
    state["d"] = state["d"][-2:] + [[i - j for i, j in zip(q, state["q"][-2])]]
    if len(state["d"]) < 3:
        return None
    dm, d, dp = state["d"]
    a = [edge_offset(*s) for s in zip(d, dm, dp)]
    last_a, state["a"] = state["a"], a
    if not last_a:
        return None
    b = [i - j for i, j in zip(last_a, dm)]
    center = state["q"][-3]
    upper = [i + limited(k, j) for i, j, k in zip(center, b, a)]
    last_upper, state["upper"] = state["upper"], upper
    if not last_upper:
        return None
    lower = [i + limited(j, k) for i, j, k in zip(center, b, a)]
    flux = hll_flux(last_upper, lower, 1)
    last_flux, state["flux"] = state["flux"], flux
    if not last_flux:
        return None
    old = before_update()
    return [i - ratio * (j - k) for i, j, k in zip(old, flux, last_flux)]


def signal_speed(u):
    density, mx, my, mz, energy = u
    inverse = 1.0 / density
    vx, vy, vz = mx * inverse, my * inverse, mz * inverse
    pressure = (adiabatic - 1.0) * (energy - 0.5 * (mx * vx + my * vy + mz * vz))
    return jnp.abs(vx) + jnp.abs(vy) + 2.0 * jnp.sqrt(adiabatic * pressure * inverse)


def inner_kernel(ratio_ref, c_ref, o_ref, edge_ref, speed_ref, ax_ref):
    groups, tiles = c_ref.shape[1], c_ref.shape[2]
    count = groups * rows
    ratio = ratio_ref[0, 0]
    up, down = tile_shifts(tiles)

    def sweep_group(g, carry):
        u = [[c_ref[f, g, t] for t in range(tiles)] for f in range(fields)]
        out = x_sweep(u, ratio, up, down)
        for f in range(fields):
            for t in range(tiles):
                ax_ref[f, g, t] = out[f][t]
        return carry

    lax.fori_loop(0, groups, sweep_group, 0)

    def row(r):
        return [ax_ref[f, r // rows, :, r % rows, :] for f in range(fields)]

    state = new_march()
    best = jnp.zeros((rows, lanes), jnp.float32)
    for r in range(count):
        u = row(r)
        at = r if r < 6 else (r - count + 12 if r >= count - 6 else None)
        if at is not None:
            for f in range(fields):
                edge_ref[f, at] = u[f]
        new = march(state, u, lambda: row(r - 3), ratio)
        if new is not None:
            p = r - 3
            for f in range(fields):
                o_ref[f, p // rows, :, p % rows, :] = new[f]
            best = jnp.maximum(best, signal_speed(new))
    speed_ref[...] = best


def outer_kernel(
    place_ref, ratio_ref, below_ref, above_ref, edge_ref, speed_ref, old_ref, o_ref, top_ref, new_ref, sem
):
    ratio = ratio_ref[0, 0]
    up, down = row_shifts()
    groups = o_ref.shape[1]
    best = speed_ref[...]
    copies = []
    for side in range(2):
        inside = [[edge_ref[f, 6 * side + r] for f in range(fields)] for r in range(6)]
        halo_ref = above_ref if side else below_ref
        end = inside[5] if side else inside[0]
        at_end = place_ref[0, side] == 1
        outside = []
        for r in range(3):
            swept = x_sweep_row([halo_ref[f, r] for f in range(fields)], ratio, up, down)
            outside.append([jnp.where(at_end, e, s) for e, s in zip(end, swept)])
        line = inside + outside if side else outside + inside
        state = new_march()
        for r in range(9):
            new = march(state, line[r], lambda: line[r - 3], ratio)
            if new is None:
                continue
            p = r - 6
            g, s = (groups - 1, 5 + p) if side else (0, p)
            for f in range(fields):
                new_ref[f, side * 3 + p] = new[f]
            copy = pltpu.make_async_copy(
                new_ref.at[:, side * 3 + p], o_ref.at[:, g, :, s, :], sem.at[side * 3 + p]
            )
            copy.start()
            copies.append(copy)
            best = jnp.maximum(best, signal_speed(new))
    best = jnp.max(best, axis=0, keepdims=True)
    top_ref[...] = jnp.broadcast_to(best, top_ref.shape)
    for copy in copies:
        copy.wait()


def groups_of(sizes, dims):
    strides = []
    total = 1
    for size in reversed(sizes):
        strides.insert(0, total)
        total *= size
    def span(ds):
        out = [0]
        for d in ds:
            out = [i + k * strides[d] for i in out for k in range(sizes[d])]
        return out
    rest = [d for d in range(len(sizes)) if d not in dims]
    return [[i + j for j in span(dims)] for i in span(rest)]


def spread_max(best, names, groups):
    got = lax.all_to_all(best[:, None, :], names, 0, 0, axis_index_groups=groups)
    return jnp.max(got, axis=(0, 1))


def body(conserved, step_ratio, *, plane_count, line_count):
    names = ("planes", "lines")
    shape = conserved.shape
    row_groups, tiles = shape[2] // rows, shape[3] // lanes
    c = conserved.reshape(fields, row_groups, rows, tiles, lanes).transpose(0, 1, 3, 2, 4)
    ratio = step_ratio.reshape(1, 1)
    low = c[:, 0, :, 0:3, :].transpose(0, 2, 1, 3)
    high = c[:, row_groups - 1, :, rows - 3 : rows, :].transpose(0, 2, 1, 3)
    below = lax.ppermute(high, "lines", [(i, i + 1) for i in range(line_count - 1)])
    above = lax.ppermute(low, "lines", [(i + 1, i) for i in range(line_count - 1)])
    vmem, smem, anywhere = (
        pl.BlockSpec(memory_space=pltpu.VMEM),
        pl.BlockSpec(memory_space=pltpu.SMEM),
        pl.BlockSpec(memory_space=pl.ANY),
    )
    f32 = jnp.float32
    inner, edge, speed = pl.pallas_call(
        inner_kernel,
        out_shape=[
            jax.ShapeDtypeStruct(c.shape, f32),
            jax.ShapeDtypeStruct((fields, 12, tiles, lanes), f32),
            jax.ShapeDtypeStruct((rows, lanes), f32),
        ],
        in_specs=[smem, vmem],
        out_specs=[vmem] * 3,
        scratch_shapes=[pltpu.VMEM(c.shape, f32)],
        compiler_params=pltpu.CompilerParams(vmem_limit_bytes=24 * 1024 * 1024),
        cost_estimate=pl.CostEstimate(flops=20_000_000, bytes_accessed=1_400_000, transcendentals=500_000),
    )(ratio, c)
    line = lax.axis_index("lines")
    place = jnp.stack([line == 0, line == line_count - 1]).astype(jnp.int32).reshape(1, 2)
    first_groups = groups_of((8, 4, 2, 2, 4), (2, 3, 4))
    second_groups = groups_of((8, 4, 2, 2, 4), (0, 1))
    advanced, top = pl.pallas_call(
        outer_kernel,
        out_shape=[
            jax.ShapeDtypeStruct(c.shape, f32),
            jax.ShapeDtypeStruct((len(first_groups[0]), lanes), f32),
        ],
        in_specs=[smem, smem, vmem, vmem, vmem, vmem, anywhere],
        out_specs=[anywhere, vmem],
        scratch_shapes=[pltpu.VMEM((fields, 6, tiles, lanes), f32), pltpu.SemaphoreType.DMA((6,))],
        input_output_aliases={6: 0},
        compiler_params=pltpu.CompilerParams(vmem_limit_bytes=24 * 1024 * 1024),
    )(place, ratio, below, above, edge, speed, inner)
    top = spread_max(top, names, first_groups)
    top = jnp.broadcast_to(top[None, :], (len(second_groups[0]), lanes))
    top = jnp.max(spread_max(top, names, second_groups))
    step_margin = safety / (step_ratio * top)
    return (advanced.transpose(0, 1, 3, 2, 4).reshape(shape), step_margin)


def solution(mesh):
    in_specs = (P(None, "planes", "lines", None), P())
    out_specs = (P(None, "planes", "lines", None), P())
    run = functools.partial(
        body, plane_count=mesh.shape["planes"], line_count=mesh.shape["lines"]
    )
    return jax.shard_map(run, mesh=mesh, in_specs=in_specs, out_specs=out_specs, check_vma=False)
```

time: 173 us -> 63.5 us (0.37)
  blocking collectives: 132 us -> 39.4 us
  other arithmetic: 20.3 us -> 0.71 us
  local copies, waits for them, and re-layouts: 18.7 us -> 1.29 us
  Pallas kernels: 0 us -> 12.6 us
  starting transfers between devices: 0 us -> 6 us
    pmin x1 -> x0, blocking collectives: 107 us -> none  [body(): step_margin = lax.pmin(local_margin, ('planes', 'lines'))]
    all_to_all x2, blocking collectives: 24.6 us -> 39.4 us  [spread_max(): lax.all_to_all(best[:, None, :], names, 0, 0, axis_index_groups=groups)]
    pallas_call x0 -> x2, Pallas kernels: none -> 12.6 us  [the longest x1 10.3 us: body(): pl.pallas_call(inner_kernel, out_shape=[jax.ShapeDtypeStruct(c.shape, f32...]
    unnamed x9 -> x0, other arithmetic: 11.2 us -> none
    unnamed x8 -> x3, local copies, waits for them, and re-layouts: 9.68 us -> 1.21 us
    ppermute x0 -> x2, starting transfers between devices: none -> 6 us  [the longest x1 4.58 us: body(): lax.ppermute(high, 'lines', [(i, i + 1) for i in range(line_count - 1)])]
    all_to_all x4 -> x0, local copies, waits for them, and re-layouts: 3.66 us -> none  [the longest x2 3.24 us: body(): lax.all_to_all(x_swept, 'lines', split_axis=3, concat_axis=2, tiled=True)]
    mul x6 -> x0, other arithmetic: 2.82 us -> none  [the longest x4 2.67 us: hll_flux(): (fastest * left_flux[component] - slowest * right_flux[component] + slowe...]
  transfers between devices with their start and end apart: 0 -> 2, of which waited for: 0 -> 0; matrix products, arithmetic and copies ran while one was open for 0% -> 0% of each run, Pallas kernels for 0% -> 16%
where the time goes in v1:
time: 63.5 us; the launch traced here: 63.2 us
  blocking collectives  39.4 us (62%)
  Pallas kernels  12.6 us (20%)
  starting transfers between devices  6 us (9%)
  between operations  3.16 us (5%)
  local copies, waits for them, and re-layouts  1.29 us (2%)
  other arithmetic  0.71 us (1%)
    all_to_all x2, blocking collectives, spread_max(): lax.all_to_all(best[:, None, :], names, 0, 0, axis_index_groups=groups)  39.4 us
    pallas_call x1, Pallas kernels, body(): pl.pallas_call(inner_kernel, out_shape=[jax.ShapeDtypeStruct(c.shape, f32...  10.3 us
    ppermute x1, starting transfers between devices, body(): lax.ppermute(high, 'lines', [(i, i + 1) for i in range(line_count - 1)])  4.58 us
    pallas_call x1, Pallas kernels, body(): pl.pallas_call(outer_kernel, out_shape=[jax.ShapeDtypeStruct(c.shape, f32...  2.27 us
    ppermute x1, starting transfers between devices, body(): lax.ppermute(low, 'lines', [(i + 1, i) for i in range(line_count - 1)])  1.42 us
  transfers between devices with their start and end apart: 2, of which 0 were waited for; matrix products, arithmetic and copies ran while one was open for 0% of the time, Pallas kernels for 16%

profile of v1, /device:TPU:1, one launch (start us, length us, event | category | flops | bytes accessed | tf_op | source)
XLA Modules:
  0.0 63.2 jit_solution(3694552913652632130)
XLA Ops:
  0.6 1.2 %copy.19 = f32[20,8,8,128]{3,2,1,0:T(8,128)S(1)} copy(f32[20,8,8,128]{3,1,2,0:T(8,128)} %bitcast.32) | data formatting | bytes 1310720
  1.8 0.0 copy-start
  1.9 0.1 copy.22
  1.9 1.4 %collective-permute-start.1 = (f32[5,3,8,128]{3,2,1,0:T(8,128)S(1)}, f32[5,3,8,128]{3,2,1,0:T(8,128)S(1)}, u32[]{:S(2)}, u32[]{:S(2)}) collective-permute-start(f32[5,3,8,128]{3,2,1,0:T(8,128)S(1)} %get-tuple-element.12), channel_id=1, source_target_pairs={{1,0},{2,1},{3,2},{4,3},{5,4},{6,5},{7,6},{9,8},{10,9},{11,10},{12... | collective-permute-start | bytes 184328 | tf_op jit(solution)/shard_map/ppermute | solution.py:299
  3.4 4.6 %collective-permute-start = (f32[5,3,8,128]{3,2,1,0:T(8,128)S(1)}, f32[5,3,8,128]{3,2,1,0:T(8,128)S(1)}, u32[]{:S(2)}, u32[]{:S(2)}) collective-permute-start(f32[5,3,8,128]{3,2,1,0:T(8,128)S(1)} %get-tuple-element.13), channel_id=1, source_target_pairs={{0,1},{1,2},{2,3},{3,4},{4,5},{5,6},{6,7},{8,9},{9,10},{10,11},{11... | collective-permute-start | bytes 184328 | tf_op jit(solution)/shard_map/ppermute | solution.py:298
  8.6 0.0 copy-done
  8.6 10.3 %shard_map.41 = (f32[5,4,8,8,128]{4,3,2,1,0:T(8,128)}, f32[5,12,8,128]{3,2,1,0:T(8,128)S(1)}, f32[8,128]{1,0:T(8,128)S(1)}) custom-call(f32[1,1]{1,0:T(1,128)} %bitcast.30.ratio_ref, f32[5,4,8,8,128]{4,3,2,1,0:T(8,128)S(1)} %bitcast.33), custom_call_target="tpu_custom_call" | custom-call | flops 20000000 | bytes 1400000 | tf_op jit(solution)/shard_map/pallas_call | solution.py:306
  18.9 0.1 add_convert_fusion.place_ref
  19.0 0.0 collective-permute-done.1.above_ref
  19.0 0.0 collective-permute-done.below_ref
  19.0 2.3 %shard_map.42 = (f32[5,4,8,8,128]{4,3,2,1,0:T(8,128)}, f32[16,128]{1,0:T(8,128)S(1)}) custom-call(s32[1,2]{1,0:T(1,128)S(1)} %add_convert_fusion.place_ref, f32[1,1]{1,0:T(1,128)} %bitcast.31.ratio_ref, f32[5,3,8,128]{3,2,1,0:T(8,128)S(1)} %collective-permute-done.below_ref, ...), custom_call_target="tpu_custom_call", output_to_operand_aliasing={{0}: (6, {})} | custom-call | tf_op jit(solution)/shard_map/pallas_call | solution.py:323
  21.3 14.8 %all_to_all.10 = f32[16,1,128]{2,1,0:T(1,128)S(1)} all-to-all(f32[16,1,128]{2,1,0:T(1,128)S(1)} %bitcast.34), channel_id=1, replica_groups={{0,1,2,3,4,5,6,7,8,9,10,11,12,13,14,15},{16,17,18,19,20,21,22,23,24,25,..., dimensions={0} | all-to-all | bytes 16384 | tf_op jit(solution)/shard_map/all_to_all | solution.py:286
  36.1 24.6 %all_to_all.11 = f32[32,1,128]{2,1,0:T(1,128)S(1)} all-to-all(f32[32,1,128]{2,1,0:T(1,128)S(1)} %broadcast_in_dim_broadcast_in_dim.2), channel_id=1, replica_groups={{0,16,32,48,64,80,96,112,128,144,160,176,192,208,224,240,256,272,288,30..., dimensions={0} | all-to-all | bytes 32768 | tf_op jit(solution)/shard_map/all_to_all | solution.py:286
  60.8 0.6 reduce_max.20
  (3 shorter events, 0.1 us)
Async XLA Ops:
  1.8 6.8 %copy-start = (f32[5,1,32,1024]{3,2,1,0:T(8,128)S(1)}, f32[5,1,32,1024]{3,2,1,0:T(8,128)}, u32[]{:S(2)}) copy-start(f32[5,1,32,1024]{3,2,1,0:T(8,128)} %param.2) | copy-start | bytes 1966084
  1.9 17.1 %collective-permute-start.1 = (f32[5,3,8,128]{3,2,1,0:T(8,128)S(1)}, f32[5,3,8,128]{3,2,1,0:T(8,128)S(1)}, u32[]{:S(2)}, u32[]{:S(2)}) collective-permute-start(f32[5,3,8,128]{3,2,1,0:T(8,128)S(1)} %get-tuple-element.12), channel_id=1, source_target_pairs={{1,0},{2,1},{3,2},{4,3},{5,4},{6,5},{7,6},{9,8},{10,9},{11,10},{12... | collective-permute-start | bytes 184328 | tf_op jit(solution)/shard_map/ppermute | solution.py:299
  3.4 15.7 %collective-permute-start = (f32[5,3,8,128]{3,2,1,0:T(8,128)S(1)}, f32[5,3,8,128]{3,2,1,0:T(8,128)S(1)}, u32[]{:S(2)}, u32[]{:S(2)}) collective-permute-start(f32[5,3,8,128]{3,2,1,0:T(8,128)S(1)} %get-tuple-element.13), channel_id=1, source_target_pairs={{0,1},{1,2},{2,3},{3,4},{4,5},{5,6},{6,7},{8,9},{9,10},{10,11},{11... | collective-permute-start | bytes 184328 | tf_op jit(solution)/shard_map/ppermute | solution.py:298

commit v2 on v1

--- a/solution.py
+++ b/solution.py
@@ -98,6 +98,7 @@
             flux[f].append(got[f])
     first = own_flux([q[v][0] for v in range(fields)], 0)
     out = []
+    ratio = ratio() if callable(ratio) else ratio
     for f in range(fields):
         before = shift_down(flux[f], [first[f]] * count)
         out.append([i - ratio * (j - k) for i, j, k in zip(u[f], flux[f], before)])
@@ -124,34 +125,6 @@
     return up, down
 
 
-def row_shifts():
-    lane = lax.broadcasted_iota(jnp.int32, (rows, lanes), 1)
-    place = lane + lanes * lax.broadcasted_iota(jnp.int32, (rows, lanes), 0)
-
-    def up(tiles, end):
-        out = []
-        for t, e in zip(tiles, end):
-            turned = pltpu.roll(t, lanes - 1, 1)
-            turned = jnp.where(lane == lanes - 1, pltpu.roll(turned, rows - 1, 0), turned)
-            out.append(jnp.where(place == rows * lanes - 1, e, turned))
-        return out
-
-    def down(tiles, end):
-        out = []
-        for t, e in zip(tiles, end):
-            turned = pltpu.roll(t, 1, 1)
-            turned = jnp.where(lane == 0, pltpu.roll(turned, 1, 0), turned)
-            out.append(jnp.where(place == 0, e, turned))
-        return out
-
-    return up, down
-
-
-def x_sweep_row(u, ratio, up, down):
-    out = x_sweep([[value] for value in u], ratio, up, down)
-    return [value[0] for value in out]
-
-
 def new_march():
     return dict(q=[], d=[], a=[], upper=[], flux=[])
 
@@ -192,76 +165,133 @@
     return jnp.abs(vx) + jnp.abs(vy) + 2.0 * jnp.sqrt(adiabatic * pressure * inverse)
 
 
-def inner_kernel(ratio_ref, c_ref, o_ref, edge_ref, speed_ref, ax_ref):
-    groups, tiles = c_ref.shape[1], c_ref.shape[2]
-    count = groups * rows
-    ratio = ratio_ref[0, 0]
+def row_at(r):
+    return pl.ds(pl.multiple_of(r * rows, rows), rows)
+
+
+def load_kernel(c_ref, in_ref, low_ref, high_ref, sem):
+    tiles, block = rows, rows * rows
+    last = c_ref.shape[1] - block
+    spans = [pl.ds(0, block), pl.ds(last, block), pl.ds(block, last - block)]
+    copies = [
+        pltpu.make_async_copy(c_ref.at[:, span, :], in_ref.at[:, span, :], sem.at[k])
+        for k, span in enumerate(spans)
+    ]
+    for copy in copies:
+        copy.start()
+    for k, (start, out_ref) in enumerate(((0, low_ref), (last + rows - ghosts, high_ref))):
+        copies[k].wait()
+        for f in range(fields):
+            for r in range(ghosts):
+                out_ref[f, pl.ds(r * tiles, tiles), :] = in_ref[f, pl.ds(start + r, tiles, stride=rows), :]
+    copies[2].wait()
+
+
+def inner_kernel(given_ref, c_ref, ax_ref, o_ref, speed_ref, ratio_ref, scalar_ref, sem):
+    tiles, count = rows, c_ref.shape[1] // rows
+    fetch = pltpu.make_async_copy(given_ref, scalar_ref, sem)
+    fetch.start()
     up, down = tile_shifts(tiles)
 
     def sweep_group(g, carry):
-        u = [[c_ref[f, g, t] for t in range(tiles)] for f in range(fields)]
+        def ratio():
+            pl.when(g == 0)(fetch.wait)
+            return scalar_ref[0, 0]
+
+        base = pl.multiple_of(g * rows * tiles, rows * tiles)
+        u = [[c_ref[f, pl.ds(base + t * rows, rows), :] for t in range(tiles)] for f in range(fields)]
         out = x_sweep(u, ratio, up, down)
         for f in range(fields):
             for t in range(tiles):
-                ax_ref[f, g, t] = out[f][t]
+                ax_ref[f, pl.ds(base + t, rows, stride=tiles), :] = out[f][t]
         return carry
 
-    lax.fori_loop(0, groups, sweep_group, 0)
+    lax.fori_loop(0, count // rows, sweep_group, 0)
+    ratio = scalar_ref[0, 0]
+    ratio_ref[...] = jnp.full((rows, lanes), ratio)
 
     def row(r):
-        return [ax_ref[f, r // rows, :, r % rows, :] for f in range(fields)]
-
-    state = new_march()
-    best = jnp.zeros((rows, lanes), jnp.float32)
-    for r in range(count):
-        u = row(r)
-        at = r if r < 6 else (r - count + 12 if r >= count - 6 else None)
-        if at is not None:
+        return [ax_ref[f, row_at(r), :] for f in range(fields)]
+
+    q = primitive(row(0))
+    zero = [jnp.zeros((rows, lanes), jnp.float32)] * fields
+    chunk = 4
+
+    def advance(i, carry):
+        q2, q1, d2, d1, a, upper, flux, best = carry
+        state = dict(q=[q2, q1], d=[d2, d1], a=a, upper=upper, flux=flux)
+        for k in range(chunk):
+            r = i * chunk + k
+            p = jnp.maximum(r - ghosts, 0)
+            new = march(state, row(r), lambda: row(p), ratio)
+            at = (p // rows) * rows * tiles + p % rows
             for f in range(fields):
-                edge_ref[f, at] = u[f]
-        new = march(state, u, lambda: row(r - 3), ratio)
-        if new is not None:
-            p = r - 3
-            for f in range(fields):
-                o_ref[f, p // rows, :, p % rows, :] = new[f]
-            best = jnp.maximum(best, signal_speed(new))
-    speed_ref[...] = best
+                o_ref[f, pl.ds(at, rows, stride=tiles), :] = new[f]
+            best = jnp.maximum(best, jnp.where(r >= 2 * ghosts, signal_speed(new), 0.0))
+        q, d = state["q"], state["d"]
+        return (q[-2], q[-1], d[-2], d[-1], state["a"], state["upper"], state["flux"], best)
+
+    done = lax.fori_loop(0, count // chunk, advance, (q, q, zero, zero, zero, q, zero, zero[0]))
+    speed_ref[...] = done[-1]
 
 
 def outer_kernel(
-    place_ref, ratio_ref, below_ref, above_ref, edge_ref, speed_ref, old_ref, o_ref, top_ref, new_ref, sem
+    place_ref, ratio_ref, below_ref, above_ref, ax_ref, inner_ref, speed_ref, o_ref, top_ref, halo_ref, side_ref, sem
 ):
-    ratio = ratio_ref[0, 0]
-    up, down = row_shifts()
-    groups = o_ref.shape[1]
+    ratio = ratio_ref[...]
+    tiles, block = rows, rows * rows
+    count = ax_ref.shape[1] // rows
+    last = ax_ref.shape[1] - block
+    middle = pltpu.make_async_copy(
+        inner_ref.at[:, pl.ds(block, last - block), :], o_ref.at[:, pl.ds(block, last - block), :], sem.at[0]
+    )
+    middle.start()
+    edge = ghosts * tiles
+    u = [[], [], [], [], []]
+    for f in range(fields):
+        halo_ref[f, pl.ds(0, edge), :] = below_ref[f]
+        halo_ref[f, pl.ds(edge, edge), :] = above_ref[f]
+        halo_ref[f, pl.ds(2 * edge, block - 2 * edge), :] = above_ref[f, pl.ds(0, block - 2 * edge), :]
+        u[f] = [halo_ref[f, pl.ds(t, rows, stride=tiles), :] for t in range(tiles)]
+    out = x_sweep(u, ratio, *tile_shifts(tiles))
+    for f in range(fields):
+        for t in range(tiles):
+            halo_ref[f, pl.ds(t, rows, stride=tiles), :] = out[f][t]
     best = speed_ref[...]
-    copies = []
+    copies = [middle]
     for side in range(2):
-        inside = [[edge_ref[f, 6 * side + r] for f in range(fields)] for r in range(6)]
-        halo_ref = above_ref if side else below_ref
+        start = last if side else 0
+        side_ref[side] = inner_ref[:, pl.ds(start, block), :]
+        first = count - 6 if side else 0
+        inside = [
+            [ax_ref[f, pl.ds((first + r) * rows, rows), :] for f in range(fields)] for r in range(6)
+        ]
         end = inside[5] if side else inside[0]
         at_end = place_ref[0, side] == 1
-        outside = []
-        for r in range(3):
-            swept = x_sweep_row([halo_ref[f, r] for f in range(fields)], ratio, up, down)
-            outside.append([jnp.where(at_end, e, s) for e, s in zip(end, swept)])
+        outside = [
+            [
+                jnp.where(at_end, end[f], halo_ref[f, pl.ds((side * ghosts + r) * tiles, tiles), :])
+                for f in range(fields)
+            ]
+            for r in range(ghosts)
+        ]
         line = inside + outside if side else outside + inside
         state = new_march()
+        speeds = []
         for r in range(9):
-            new = march(state, line[r], lambda: line[r - 3], ratio)
+            new = march(state, line[r], lambda: line[r - ghosts], ratio)
             if new is None:
                 continue
-            p = r - 6
-            g, s = (groups - 1, 5 + p) if side else (0, p)
+            p = r - 6 + (rows - ghosts if side else 0)
             for f in range(fields):
-                new_ref[f, side * 3 + p] = new[f]
-            copy = pltpu.make_async_copy(
-                new_ref.at[:, side * 3 + p], o_ref.at[:, g, :, s, :], sem.at[side * 3 + p]
-            )
-            copy.start()
-            copies.append(copy)
+                side_ref[side, f, pl.ds(p, rows, stride=tiles), :] = new[f]
             best = jnp.maximum(best, signal_speed(new))
-    best = jnp.max(best, axis=0, keepdims=True)
+        copy = pltpu.make_async_copy(
+            side_ref.at[side], o_ref.at[:, pl.ds(start, block), :], sem.at[1 + side]
+        )
+        copy.start()
+        copies.append(copy)
+    best = jnp.max(ratio * best, axis=0, keepdims=True)
     top_ref[...] = jnp.broadcast_to(best, top_ref.shape)
     for copy in copies:
         copy.wait()
@@ -282,60 +312,66 @@
     return [[i + j for j in span(dims)] for i in span(rest)]
 
 
-def spread_max(best, names, groups):
-    got = lax.all_to_all(best[:, None, :], names, 0, 0, axis_index_groups=groups)
-    return jnp.max(got, axis=(0, 1))
+def gather_all(best, names, groups):
+    return lax.all_to_all(best[:, None, :], names, 0, 0, axis_index_groups=groups)
 
 
 def body(conserved, step_ratio, *, plane_count, line_count):
     names = ("planes", "lines")
     shape = conserved.shape
-    row_groups, tiles = shape[2] // rows, shape[3] // lanes
-    c = conserved.reshape(fields, row_groups, rows, tiles, lanes).transpose(0, 1, 3, 2, 4)
-    ratio = step_ratio.reshape(1, 1)
-    low = c[:, 0, :, 0:3, :].transpose(0, 2, 1, 3)
-    high = c[:, row_groups - 1, :, rows - 3 : rows, :].transpose(0, 2, 1, 3)
-    below = lax.ppermute(high, "lines", [(i, i + 1) for i in range(line_count - 1)])
-    above = lax.ppermute(low, "lines", [(i + 1, i) for i in range(line_count - 1)])
-    vmem, smem, anywhere = (
+    groups, tiles = shape[2] // rows, shape[3] // lanes
+    c = conserved.reshape(fields, groups, rows, tiles, lanes).transpose(0, 1, 3, 2, 4)
+    c = c.reshape(fields, groups * tiles * rows, lanes)
+    vmem, smem, anywhere, hbm = (
         pl.BlockSpec(memory_space=pltpu.VMEM),
         pl.BlockSpec(memory_space=pltpu.SMEM),
         pl.BlockSpec(memory_space=pl.ANY),
+        pl.BlockSpec(memory_space=pltpu.HBM),
     )
     f32 = jnp.float32
-    inner, edge, speed = pl.pallas_call(
+    whole = jax.ShapeDtypeStruct(c.shape, f32)
+    edge = jax.ShapeDtypeStruct((fields, ghosts * tiles, lanes), f32)
+    params = pltpu.CompilerParams(vmem_limit_bytes=24 * 1024 * 1024)
+    own, low, high = pl.pallas_call(
+        load_kernel,
+        out_shape=[whole, edge, edge],
+        in_specs=[hbm],
+        out_specs=[vmem] * 3,
+        scratch_shapes=[pltpu.SemaphoreType.DMA((3,))],
+        compiler_params=params,
+    )(c)
+    below = lax.ppermute(high, "lines", [(i, i + 1) for i in range(line_count - 1)])
+    above = lax.ppermute(low, "lines", [(i + 1, i) for i in range(line_count - 1)])
+    tile = jax.ShapeDtypeStruct((rows, lanes), f32)
+    after_x, inner, speed, ratio = pl.pallas_call(
         inner_kernel,
-        out_shape=[
-            jax.ShapeDtypeStruct(c.shape, f32),
-            jax.ShapeDtypeStruct((fields, 12, tiles, lanes), f32),
-            jax.ShapeDtypeStruct((rows, lanes), f32),
-        ],
-        in_specs=[smem, vmem],
-        out_specs=[vmem] * 3,
-        scratch_shapes=[pltpu.VMEM(c.shape, f32)],
-        compiler_params=pltpu.CompilerParams(vmem_limit_bytes=24 * 1024 * 1024),
+        out_shape=[whole, whole, tile, tile],
+        in_specs=[hbm, vmem],
+        out_specs=[vmem] * 4,
+        scratch_shapes=[pltpu.SMEM((1, 1), f32), pltpu.SemaphoreType.DMA],
+        compiler_params=params,
         cost_estimate=pl.CostEstimate(flops=20_000_000, bytes_accessed=1_400_000, transcendentals=500_000),
-    )(ratio, c)
+    )(step_ratio.reshape(1, 1), own)
     line = lax.axis_index("lines")
     place = jnp.stack([line == 0, line == line_count - 1]).astype(jnp.int32).reshape(1, 2)
-    first_groups = groups_of((8, 4, 2, 2, 4), (2, 3, 4))
-    second_groups = groups_of((8, 4, 2, 2, 4), (0, 1))
+    first_groups = groups_of((8, 4, 2, 2, 4), (1, 2, 3))
+    second_groups = groups_of((8, 4, 2, 2, 4), (0, 4))
     advanced, top = pl.pallas_call(
         outer_kernel,
-        out_shape=[
-            jax.ShapeDtypeStruct(c.shape, f32),
-            jax.ShapeDtypeStruct((len(first_groups[0]), lanes), f32),
+        out_shape=[whole, jax.ShapeDtypeStruct((len(first_groups[0]), lanes), f32)],
+        in_specs=[smem] + [vmem] * 6,
+        out_specs=[anywhere, vmem],
+        scratch_shapes=[
+            pltpu.VMEM((fields, rows * rows, lanes), f32),
+            pltpu.VMEM((2, fields, rows * rows, lanes), f32),
+            pltpu.SemaphoreType.DMA((3,)),
         ],
-        in_specs=[smem, smem, vmem, vmem, vmem, vmem, anywhere],
-        out_specs=[anywhere, vmem],
-        scratch_shapes=[pltpu.VMEM((fields, 6, tiles, lanes), f32), pltpu.SemaphoreType.DMA((6,))],
-        input_output_aliases={6: 0},
-        compiler_params=pltpu.CompilerParams(vmem_limit_bytes=24 * 1024 * 1024),
-    )(place, ratio, below, above, edge, speed, inner)
-    top = spread_max(top, names, first_groups)
+        compiler_params=params,
+    )(place, ratio, below, above, after_x, inner, speed)
+    advanced = advanced.reshape(fields, groups, tiles, rows, lanes)
+    top = jnp.max(gather_all(top, names, first_groups), axis=(0, 1))
     top = jnp.broadcast_to(top[None, :], (len(second_groups[0]), lanes))
-    top = jnp.max(spread_max(top, names, second_groups))
-    step_margin = safety / (step_ratio * top)
+    step_margin = jnp.min(safety / gather_all(top, names, second_groups))
     return (advanced.transpose(0, 1, 3, 2, 4).reshape(shape), step_margin)
 
 

time: 63.5 us -> 52 us (0.82)
  Pallas kernels: 12.6 us -> 5.83 us
  blocking collectives: 39.4 us -> 37.5 us
  between operations: 3.16 us -> 1.34 us
  starting transfers between devices: 6 us -> 5.24 us
    pallas_call x2 -> x3, Pallas kernels: 12.6 us -> 5.83 us  [the longest x1 3.6 us: body(): pl.pallas_call(inner_kernel, out_shape=[whole, whole, tile, tile], in_spe...]
    all_to_all x2, blocking collectives: 39.4 us -> 37.5 us  [gather_all(): lax.all_to_all(best[:, None, :], names, 0, 0, axis_index_groups=groups)]
  transfers between devices with their start and end apart: 2 -> 2, of which waited for: 0 -> 0; matrix products, arithmetic and copies ran while one was open for 0% -> 0% of each run, Pallas kernels for 16% -> 7%
where the time goes in v2:
time: 52 us; the launch traced here: 51.8 us
  blocking collectives  37.5 us (72%)
  Pallas kernels  5.83 us (11%)
  starting transfers between devices  5.24 us (10%)
  between operations  1.34 us (3%)
  local copies, waits for them, and re-layouts  1.09 us (2%)
  other arithmetic  0.72 us (1%)
    all_to_all x2, blocking collectives, gather_all(): lax.all_to_all(best[:, None, :], names, 0, 0, axis_index_groups=groups)  37.5 us
    ppermute x1, starting transfers between devices, body(): lax.ppermute(high, 'lines', [(i, i + 1) for i in range(line_count - 1)])  3.95 us
    pallas_call x1, Pallas kernels, body(): pl.pallas_call(inner_kernel, out_shape=[whole, whole, tile, tile], in_spe...  3.6 us
    pallas_call x1, Pallas kernels, body(): pl.pallas_call(outer_kernel, out_shape=[whole, jax.ShapeDtypeStruct((len(...  2.08 us
    ppermute x1, starting transfers between devices, body(): lax.ppermute(low, 'lines', [(i + 1, i) for i in range(line_count - 1)])  1.29 us
    unnamed x2, local copies, waits for them, and re-layouts  1.08 us
  transfers between devices with their start and end apart: 2, of which 0 were waited for; matrix products, arithmetic and copies ran while one was open for 0% of the time, Pallas kernels for 7%

profile of v2, /device:TPU:1, one launch (start us, length us, event | category | flops | bytes accessed | tf_op | source)
XLA Modules:
  0.0 51.8 jit_solution(3764287389973239576)
XLA Ops:
  0.6 0.0 copy-start
  0.6 1.1 %copy-done = f32[5,1,32,1024]{3,2,1,0:T(8,128)S(1)} copy-done((f32[5,1,32,1024]{3,2,1,0:T(8,128)S(1)}, f32[5,1,32,1024]{3,2,1,0:T(8,128)}, u32[]{:S(2)}) %copy-start) | copy-done | bytes 655384
  1.7 0.2 shard_map.41
  1.9 3.9 %collective-permute-start = (f32[5,24,128]{2,1,0:T(8,128)S(1)}, f32[5,24,128]{2,1,0:T(8,128)S(1)}, u32[]{:S(2)}, u32[]{:S(2)}) collective-permute-start(f32[5,24,128]{2,1,0:T(8,128)S(1)} %get-tuple-element.13), channel_id=1, source_target_pairs={{0,1},{1,2},{2,3},{3,4},{4,5},{5,6},{6,7},{8,9},{9,10},{10,11},{11... | collective-permute-start | bytes 184328 | tf_op jit(solution)/shard_map/ppermute | solution.py:343
  5.8 1.3 %collective-permute-start.1 = (f32[5,24,128]{2,1,0:T(8,128)S(1)}, f32[5,24,128]{2,1,0:T(8,128)S(1)}, u32[]{:S(2)}, u32[]{:S(2)}) collective-permute-start(f32[5,24,128]{2,1,0:T(8,128)S(1)} %get-tuple-element.14), channel_id=1, source_target_pairs={{1,0},{2,1},{3,2},{4,3},{5,4},{6,5},{7,6},{9,8},{10,9},{11,10},{12... | collective-permute-start | bytes 184328 | tf_op jit(solution)/shard_map/ppermute | solution.py:344
  7.8 3.6 %shard_map.42 = (f32[5,256,128]{2,1,0:T(8,128)S(1)}, f32[5,256,128]{2,1,0:T(8,128)S(1)}, f32[8,128]{1,0:T(8,128)S(1)}, f32[8,128]{1,0:T(8,128)S(1)}) custom-call(f32[1,1]{1,0:T(1,128)} %bitcast.17.given_ref, f32[5,256,128]{2,1,0:T(8,128)S(1)} %get-tuple-element.11.c_ref), custom_call_target="tpu_custom_call" | custom-call | flops 20000000 | bytes 1400000 | tf_op jit(solution)/shard_map/pallas_call | solution.py:346
  11.4 0.1 add_convert_fusion.place_ref
  11.5 0.0 collective-permute-done.below_ref
  11.5 0.0 collective-permute-done.1.above_ref
  11.5 2.1 %shard_map.43 = (f32[5,256,128]{2,1,0:T(8,128)}, f32[16,128]{1,0:T(8,128)S(1)}) custom-call(s32[1,2]{1,0:T(1,128)S(1)} %add_convert_fusion.place_ref, f32[8,128]{1,0:T(8,128)S(1)} %get-tuple-element.12.ratio_ref, f32[5,24,128]{2,1,0:T(8,128)S(1)} %collective-permute-done.below_ref, f32[5,24,128]{2,1,0:T(8,128)S(1)} %collective-permute-done.1.above_ref, ...), custom_call_target="tpu_custom_call" | custom-call | tf_op jit(solution)/shard_map/pallas_call | solution.py:359
  13.6 17.3 %all_to_all.10 = f32[16,1,128]{2,1,0:T(1,128)S(1)} all-to-all(f32[16,1,128]{2,1,0:T(1,128)S(1)} %bitcast.19), channel_id=1, replica_groups={{0,4,8,12,16,20,24,28,32,36,40,44,48,52,56,60},{1,5,9,13,17,21,25,29,33..., dimensions={0} | all-to-all | bytes 16384 | tf_op jit(solution)/shard_map/all_to_all | solution.py:316
  30.9 20.2 %all_to_all.11 = f32[32,1,128]{2,1,0:T(1,128)S(1)} all-to-all(f32[32,1,128]{2,1,0:T(1,128)S(1)} %broadcast_in_dim_broadcast_in_dim.2), channel_id=1, replica_groups={{0,1,2,3,64,65,66,67,128,129,130,131,192,193,194,195,256,257,258,259,32..., dimensions={0} | all-to-all | bytes 32768 | tf_op jit(solution)/shard_map/all_to_all | solution.py:316
  51.2 0.6 %divide_reduce_fusion = f32[]{:T(128)} fusion(f32[32,1,128]{2,0,1:T(8,128)S(1)} %bitcast.20), kind=kLoop, calls=%fused_computation | loop fusion | flops 8191 | bytes 16388 | tf_op jit(solution)/shard_map/reduce_min | solution.py:374
  (2 shorter events, 0.0 us)
Async XLA Ops:
  0.6 1.1 %copy-start = (f32[5,1,32,1024]{3,2,1,0:T(8,128)S(1)}, f32[5,1,32,1024]{3,2,1,0:T(8,128)}, u32[]{:S(2)}) copy-start(f32[5,1,32,1024]{3,2,1,0:T(8,128)} %param.2) | copy-start | bytes 1966084
  1.9 9.6 %collective-permute-start = (f32[5,24,128]{2,1,0:T(8,128)S(1)}, f32[5,24,128]{2,1,0:T(8,128)S(1)}, u32[]{:S(2)}, u32[]{:S(2)}) collective-permute-start(f32[5,24,128]{2,1,0:T(8,128)S(1)} %get-tuple-element.13), channel_id=1, source_target_pairs={{0,1},{1,2},{2,3},{3,4},{4,5},{5,6},{6,7},{8,9},{9,10},{10,11},{11... | collective-permute-start | bytes 184328 | tf_op jit(solution)/shard_map/ppermute | solution.py:343
  5.8 5.6 %collective-permute-start.1 = (f32[5,24,128]{2,1,0:T(8,128)S(1)}, f32[5,24,128]{2,1,0:T(8,128)S(1)}, u32[]{:S(2)}, u32[]{:S(2)}) collective-permute-start(f32[5,24,128]{2,1,0:T(8,128)S(1)} %get-tuple-element.14), channel_id=1, source_target_pairs={{1,0},{2,1},{3,2},{4,3},{5,4},{6,5},{7,6},{9,8},{10,9},{11,10},{12... | collective-permute-start | bytes 184328 | tf_op jit(solution)/shard_map/ppermute | solution.py:344

commit v3 on v2

--- a/solution.py
+++ b/solution.py
@@ -1,7 +1,9 @@
 import functools
+import math
 
 import jax
 import jax.numpy as jnp
+import numpy as np
 from jax import lax
 from jax.experimental import pallas as pl
 from jax.experimental.pallas import tpu as pltpu
@@ -13,6 +15,7 @@
 fields = 5
 rows = 8
 lanes = 128
+sizes = (8, 4, 2, 2, 4)
 
 
 def primitive(u):
@@ -297,19 +300,14 @@
         copy.wait()
 
 
-def groups_of(sizes, dims):
-    strides = []
-    total = 1
-    for size in reversed(sizes):
-        strides.insert(0, total)
-        total *= size
-    def span(ds):
-        out = [0]
-        for d in ds:
-            out = [i + k * strides[d] for i in out for k in range(sizes[d])]
-        return out
-    rest = [d for d in range(len(sizes)) if d not in dims]
-    return [[i + j for j in span(dims)] for i in span(rest)]
+def groups_of(dims, first):
+    axes = ("z", "y_hi", "core", "y_lo", "x")
+    numbers = np.arange(math.prod(sizes)).reshape(sizes)
+    for axis, place in first.items():
+        numbers = np.roll(numbers, -place, axis=axes.index(axis))
+    order = [a for a in axes if a not in dims] + [a for a in axes if a in dims]
+    count = math.prod(sizes[axes.index(a)] for a in dims)
+    return numbers.transpose([axes.index(a) for a in order]).reshape(-1, count).tolist()
 
 
 def gather_all(best, names, groups):
@@ -354,8 +352,8 @@
     )(step_ratio.reshape(1, 1), own)
     line = lax.axis_index("lines")
     place = jnp.stack([line == 0, line == line_count - 1]).astype(jnp.int32).reshape(1, 2)
-    first_groups = groups_of((8, 4, 2, 2, 4), (1, 2, 3))
-    second_groups = groups_of((8, 4, 2, 2, 4), (0, 4))
+    first_groups = groups_of(("z", "core"), {"z": 5})
+    second_groups = groups_of(("y_hi", "y_lo", "x"), {"y_hi": 2, "x": 2})
     advanced, top = pl.pallas_call(
         outer_kernel,
         out_shape=[whole, jax.ShapeDtypeStruct((len(first_groups[0]), lanes), f32)],

time: 52 us -> 45.6 us (0.88); the launches traced: 51.8 us -> 44.8 us
  blocking collectives: 37.5 us -> 30.6 us
    all_to_all x2, blocking collectives: 37.5 us -> 30.6 us  [gather_all(): lax.all_to_all(best[:, None, :], names, 0, 0, axis_index_groups=groups)]
  transfers between devices with their start and end apart: 2 -> 2, of which waited for: 0 -> 0; matrix products, arithmetic and copies ran while one was open for 0% -> 0% of each run, Pallas kernels for 7% -> 8%
where the time goes in v3:
time: 45.6 us; the launch traced here: 44.8 us
  blocking collectives  30.6 us (67%)
  Pallas kernels  5.83 us (13%)
  starting transfers between devices  5.24 us (11%)
  between operations  1.34 us (3%)
  local copies, waits for them, and re-layouts  1.09 us (2%)
  other arithmetic  0.72 us (2%)
    all_to_all x2, blocking collectives, gather_all(): lax.all_to_all(best[:, None, :], names, 0, 0, axis_index_groups=groups)  30.6 us
    ppermute x1, starting transfers between devices, body(): lax.ppermute(high, 'lines', [(i, i + 1) for i in range(line_count - 1)])  3.95 us
    pallas_call x1, Pallas kernels, body(): pl.pallas_call(inner_kernel, out_shape=[whole, whole, tile, tile], in_spe...  3.6 us
    pallas_call x1, Pallas kernels, body(): pl.pallas_call(outer_kernel, out_shape=[whole, jax.ShapeDtypeStruct((len(...  2.08 us
    ppermute x1, starting transfers between devices, body(): lax.ppermute(low, 'lines', [(i + 1, i) for i in range(line_count - 1)])  1.29 us
    unnamed x2, local copies, waits for them, and re-layouts  1.08 us
  transfers between devices with their start and end apart: 2, of which 0 were waited for; matrix products, arithmetic and copies ran while one was open for 0% of the time, Pallas kernels for 8%

profile of v3, /device:TPU:1, one launch (start us, length us, event | category | flops | bytes accessed | tf_op | source)
XLA Modules:
  0.0 44.8 jit_solution(5903471226112863963)
XLA Ops:
  0.6 0.0 copy-start
  0.6 1.1 %copy-done = f32[5,1,32,1024]{3,2,1,0:T(8,128)S(1)} copy-done((f32[5,1,32,1024]{3,2,1,0:T(8,128)S(1)}, f32[5,1,32,1024]{3,2,1,0:T(8,128)}, u32[]{:S(2)}) %copy-start) | copy-done | bytes 655384
  1.7 0.2 shard_map.41
  1.9 3.9 %collective-permute-start = (f32[5,24,128]{2,1,0:T(8,128)S(1)}, f32[5,24,128]{2,1,0:T(8,128)S(1)}, u32[]{:S(2)}, u32[]{:S(2)}) collective-permute-start(f32[5,24,128]{2,1,0:T(8,128)S(1)} %get-tuple-element.13), channel_id=1, source_target_pairs={{0,1},{1,2},{2,3},{3,4},{4,5},{5,6},{6,7},{8,9},{9,10},{10,11},{11... | collective-permute-start | bytes 184328 | tf_op jit(solution)/shard_map/ppermute | solution.py:341
  5.8 1.3 %collective-permute-start.1 = (f32[5,24,128]{2,1,0:T(8,128)S(1)}, f32[5,24,128]{2,1,0:T(8,128)S(1)}, u32[]{:S(2)}, u32[]{:S(2)}) collective-permute-start(f32[5,24,128]{2,1,0:T(8,128)S(1)} %get-tuple-element.14), channel_id=1, source_target_pairs={{1,0},{2,1},{3,2},{4,3},{5,4},{6,5},{7,6},{9,8},{10,9},{11,10},{12... | collective-permute-start | bytes 184328 | tf_op jit(solution)/shard_map/ppermute | solution.py:342
  7.8 3.6 %shard_map.42 = (f32[5,256,128]{2,1,0:T(8,128)S(1)}, f32[5,256,128]{2,1,0:T(8,128)S(1)}, f32[8,128]{1,0:T(8,128)S(1)}, f32[8,128]{1,0:T(8,128)S(1)}) custom-call(f32[1,1]{1,0:T(1,128)} %bitcast.17.given_ref, f32[5,256,128]{2,1,0:T(8,128)S(1)} %get-tuple-element.11.c_ref), custom_call_target="tpu_custom_call" | custom-call | flops 20000000 | bytes 1400000 | tf_op jit(solution)/shard_map/pallas_call | solution.py:344
  11.4 0.1 add_convert_fusion.place_ref
  11.5 0.0 collective-permute-done.below_ref
  11.5 0.0 collective-permute-done.1.above_ref
  11.5 2.1 %shard_map.43 = (f32[5,256,128]{2,1,0:T(8,128)}, f32[16,128]{1,0:T(8,128)S(1)}) custom-call(s32[1,2]{1,0:T(1,128)S(1)} %add_convert_fusion.place_ref, f32[8,128]{1,0:T(8,128)S(1)} %get-tuple-element.12.ratio_ref, f32[5,24,128]{2,1,0:T(8,128)S(1)} %collective-permute-done.below_ref, f32[5,24,128]{2,1,0:T(8,128)S(1)} %collective-permute-done.1.above_ref, ...), custom_call_target="tpu_custom_call" | custom-call | tf_op jit(solution)/shard_map/pallas_call | solution.py:357
  13.6 16.5 %all_to_all.10 = f32[16,1,128]{2,1,0:T(1,128)S(1)} all-to-all(f32[16,1,128]{2,1,0:T(1,128)S(1)} %bitcast.19), channel_id=1, replica_groups={{320,328,384,392,448,456,0,8,64,72,128,136,192,200,256,264},{321,329,38..., dimensions={0} | all-to-all | bytes 16384 | tf_op jit(solution)/shard_map/all_to_all | solution.py:314
  30.1 14.1 %all_to_all.11 = f32[32,1,128]{2,1,0:T(1,128)S(1)} all-to-all(f32[32,1,128]{2,1,0:T(1,128)S(1)} %broadcast_in_dim_broadcast_in_dim.2), channel_id=1, replica_groups={{34,35,32,33,38,39,36,37,50,51,48,49,54,55,52,53,2,3,0,1,6,7,4,5,18,19,..., dimensions={0} | all-to-all | bytes 32768 | tf_op jit(solution)/shard_map/all_to_all | solution.py:314
  44.2 0.6 %divide_reduce_fusion = f32[]{:T(128)} fusion(f32[32,1,128]{2,0,1:T(8,128)S(1)} %bitcast.20), kind=kLoop, calls=%fused_computation | loop fusion | flops 8191 | bytes 16388 | tf_op jit(solution)/shard_map/reduce_min | solution.py:372
  (2 shorter events, 0.0 us)
Async XLA Ops:
  0.6 1.1 %copy-start = (f32[5,1,32,1024]{3,2,1,0:T(8,128)S(1)}, f32[5,1,32,1024]{3,2,1,0:T(8,128)}, u32[]{:S(2)}) copy-start(f32[5,1,32,1024]{3,2,1,0:T(8,128)} %param.2) | copy-start | bytes 1966084
  1.9 9.6 %collective-permute-start = (f32[5,24,128]{2,1,0:T(8,128)S(1)}, f32[5,24,128]{2,1,0:T(8,128)S(1)}, u32[]{:S(2)}, u32[]{:S(2)}) collective-permute-start(f32[5,24,128]{2,1,0:T(8,128)S(1)} %get-tuple-element.13), channel_id=1, source_target_pairs={{0,1},{1,2},{2,3},{3,4},{4,5},{5,6},{6,7},{8,9},{9,10},{10,11},{11... | collective-permute-start | bytes 184328 | tf_op jit(solution)/shard_map/ppermute | solution.py:341
  5.8 5.6 %collective-permute-start.1 = (f32[5,24,128]{2,1,0:T(8,128)S(1)}, f32[5,24,128]{2,1,0:T(8,128)S(1)}, u32[]{:S(2)}, u32[]{:S(2)}) collective-permute-start(f32[5,24,128]{2,1,0:T(8,128)S(1)} %get-tuple-element.14), channel_id=1, source_target_pairs={{1,0},{2,1},{3,2},{4,3},{5,4},{6,5},{7,6},{9,8},{10,9},{11,10},{12... | collective-permute-start | bytes 184328 | tf_op jit(solution)/shard_map/ppermute | solution.py:342

commit v4 on v3

--- a/solution.py
+++ b/solution.py
@@ -172,7 +172,16 @@
     return pl.ds(pl.multiple_of(r * rows, rows), rows)
 
 
-def load_kernel(c_ref, in_ref, low_ref, high_ref, sem):
+def sweep_group(read, ax_ref, to, ratio):
+    tiles = rows
+    u = [[read(f, t) for t in range(tiles)] for f in range(fields)]
+    out = x_sweep(u, ratio, *tile_shifts(tiles))
+    for f in range(fields):
+        for t in range(tiles):
+            ax_ref[f, pl.ds(to + t, rows, stride=tiles), :] = out[f][t]
+
+
+def load_kernel(c_ref, in_ref, first_ref, second_ref, sem):
     tiles, block = rows, rows * rows
     last = c_ref.shape[1] - block
     spans = [pl.ds(0, block), pl.ds(last, block), pl.ds(block, last - block)]
@@ -182,36 +191,29 @@
     ]
     for copy in copies:
         copy.start()
-    for k, (start, out_ref) in enumerate(((0, low_ref), (last + rows - ghosts, high_ref))):
-        copies[k].wait()
-        for f in range(fields):
-            for r in range(ghosts):
-                out_ref[f, pl.ds(r * tiles, tiles), :] = in_ref[f, pl.ds(start + r, tiles, stride=rows), :]
+    copies[0].wait()
+    copies[1].wait()
+    even = lax.axis_index("lines") % 2 == 0
+    for f in range(fields):
+        for r in range(ghosts):
+            low = in_ref[f, pl.ds(r, tiles, stride=rows), :]
+            high = in_ref[f, pl.ds(last + rows - ghosts + r, tiles, stride=rows), :]
+            first_ref[f, pl.ds(r * tiles, tiles), :] = jnp.where(even, high, low)
+            second_ref[f, pl.ds(r * tiles, tiles), :] = jnp.where(even, low, high)
     copies[2].wait()
 
 
-def inner_kernel(given_ref, c_ref, ax_ref, o_ref, speed_ref, ratio_ref, scalar_ref, sem):
-    tiles, count = rows, c_ref.shape[1] // rows
-    fetch = pltpu.make_async_copy(given_ref, scalar_ref, sem)
-    fetch.start()
-    up, down = tile_shifts(tiles)
-
-    def sweep_group(g, carry):
-        def ratio():
-            pl.when(g == 0)(fetch.wait)
-            return scalar_ref[0, 0]
-
-        base = pl.multiple_of(g * rows * tiles, rows * tiles)
-        u = [[c_ref[f, pl.ds(base + t * rows, rows), :] for t in range(tiles)] for f in range(fields)]
-        out = x_sweep(u, ratio, up, down)
-        for f in range(fields):
-            for t in range(tiles):
-                ax_ref[f, pl.ds(base + t, rows, stride=tiles), :] = out[f][t]
+def inner_kernel(ratio_ref, c_ref, ax_ref, o_ref, speed_ref):
+    tiles, block = rows, rows * rows
+    count = c_ref.shape[1] // rows
+    ratio = ratio_ref[...]
+
+    def sweep(g, carry):
+        base = pl.multiple_of(g * block, block)
+        sweep_group(lambda f, t: c_ref[f, pl.ds(base + t * rows, rows), :], ax_ref, base, ratio)
         return carry
 
-    lax.fori_loop(0, count // rows, sweep_group, 0)
-    ratio = scalar_ref[0, 0]
-    ratio_ref[...] = jnp.full((rows, lanes), ratio)
+    lax.fori_loop(0, count // rows, sweep, 0)
 
     def row(r):
         return [ax_ref[f, row_at(r), :] for f in range(fields)]
@@ -239,41 +241,50 @@
 
 
 def outer_kernel(
-    place_ref, ratio_ref, below_ref, above_ref, ax_ref, inner_ref, speed_ref, o_ref, top_ref, halo_ref, side_ref, sem
+    line_count, ratio_ref, first_ref, second_ref, ax_ref, inner_ref, speed_ref, o_ref, top_ref, halo_ref, side_ref, sem
 ):
     ratio = ratio_ref[...]
     tiles, block = rows, rows * rows
-    count = ax_ref.shape[1] // rows
-    last = ax_ref.shape[1] - block
+    last = inner_ref.shape[1] - block
     middle = pltpu.make_async_copy(
         inner_ref.at[:, pl.ds(block, last - block), :], o_ref.at[:, pl.ds(block, last - block), :], sem.at[0]
     )
     middle.start()
     edge = ghosts * tiles
-    u = [[], [], [], [], []]
-    for f in range(fields):
-        halo_ref[f, pl.ds(0, edge), :] = below_ref[f]
-        halo_ref[f, pl.ds(edge, edge), :] = above_ref[f]
-        halo_ref[f, pl.ds(2 * edge, block - 2 * edge), :] = above_ref[f, pl.ds(0, block - 2 * edge), :]
-        u[f] = [halo_ref[f, pl.ds(t, rows, stride=tiles), :] for t in range(tiles)]
-    out = x_sweep(u, ratio, *tile_shifts(tiles))
+    for f in range(fields):
+        halo_ref[f, pl.ds(0, edge), :] = first_ref[f]
+        halo_ref[f, pl.ds(edge, edge), :] = second_ref[f]
+        halo_ref[f, pl.ds(2 * edge, block - 2 * edge), :] = second_ref[f, pl.ds(0, block - 2 * edge), :]
+    u = [[halo_ref[f, pl.ds(t, rows, stride=tiles), :] for t in range(tiles)] for f in range(fields)]
+    swept = x_sweep(u, ratio, *tile_shifts(tiles))
     for f in range(fields):
         for t in range(tiles):
-            halo_ref[f, pl.ds(t, rows, stride=tiles), :] = out[f][t]
+            halo_ref[f, pl.ds(t, rows, stride=tiles), :] = swept[f][t]
+    place = lax.axis_index("lines")
+    even = place % 2 == 0
     best = speed_ref[...]
     copies = [middle]
     for side in range(2):
         start = last if side else 0
         side_ref[side] = inner_ref[:, pl.ds(start, block), :]
-        first = count - 6 if side else 0
+        first = ax_ref.shape[1] // tiles - 6 if side else 0
         inside = [
             [ax_ref[f, pl.ds((first + r) * rows, rows), :] for f in range(fields)] for r in range(6)
         ]
         end = inside[5] if side else inside[0]
-        at_end = place_ref[0, side] == 1
+        at_end = place == (line_count - 1 if side else 0)
+        from_first = even if side else jnp.logical_not(even)
         outside = [
             [
-                jnp.where(at_end, end[f], halo_ref[f, pl.ds((side * ghosts + r) * tiles, tiles), :])
+                jnp.where(
+                    at_end,
+                    end[f],
+                    jnp.where(
+                        from_first,
+                        halo_ref[f, pl.ds(r * tiles, tiles), :],
+                        halo_ref[f, pl.ds(edge + r * tiles, tiles), :],
+                    ),
+                )
                 for f in range(fields)
             ]
             for r in range(ghosts)
@@ -301,13 +312,18 @@
 
 
 def groups_of(dims, first):
-    axes = ("z", "y_hi", "core", "y_lo", "x")
+    axes = ("half", "depth", "y_hi", "core", "y_lo", "x")
     numbers = np.arange(math.prod(sizes)).reshape(sizes)
+    numbers = np.stack([numbers[: sizes[0] // 2], numbers[: sizes[0] // 2 - 1 : -1]])
     for axis, place in first.items():
         numbers = np.roll(numbers, -place, axis=axes.index(axis))
-    order = [a for a in axes if a not in dims] + [a for a in axes if a in dims]
-    count = math.prod(sizes[axes.index(a)] for a in dims)
-    return numbers.transpose([axes.index(a) for a in order]).reshape(-1, count).tolist()
+    order = [axes.index(a) for a in axes if a not in dims] + [axes.index(a) for a in axes if a in dims]
+    count = math.prod(numbers.shape[axes.index(a)] for a in dims)
+    return numbers.transpose(order).reshape(-1, count).tolist()
+
+
+def neighbours(start, count):
+    return [p for i in range(start, count - 1, 2) for p in ((i, i + 1), (i + 1, i))]
 
 
 def gather_all(best, names, groups):
@@ -320,9 +336,8 @@
     groups, tiles = shape[2] // rows, shape[3] // lanes
     c = conserved.reshape(fields, groups, rows, tiles, lanes).transpose(0, 1, 3, 2, 4)
     c = c.reshape(fields, groups * tiles * rows, lanes)
-    vmem, smem, anywhere, hbm = (
+    vmem, anywhere, hbm = (
         pl.BlockSpec(memory_space=pltpu.VMEM),
-        pl.BlockSpec(memory_space=pltpu.SMEM),
         pl.BlockSpec(memory_space=pl.ANY),
         pl.BlockSpec(memory_space=pltpu.HBM),
     )
@@ -330,34 +345,32 @@
     whole = jax.ShapeDtypeStruct(c.shape, f32)
     edge = jax.ShapeDtypeStruct((fields, ghosts * tiles, lanes), f32)
     params = pltpu.CompilerParams(vmem_limit_bytes=24 * 1024 * 1024)
-    own, low, high = pl.pallas_call(
+    tile = jax.ShapeDtypeStruct((rows, lanes), f32)
+    own, first, second = pl.pallas_call(
         load_kernel,
         out_shape=[whole, edge, edge],
         in_specs=[hbm],
         out_specs=[vmem] * 3,
         scratch_shapes=[pltpu.SemaphoreType.DMA((3,))],
         compiler_params=params,
-    )(c)
-    below = lax.ppermute(high, "lines", [(i, i + 1) for i in range(line_count - 1)])
-    above = lax.ppermute(low, "lines", [(i + 1, i) for i in range(line_count - 1)])
-    tile = jax.ShapeDtypeStruct((rows, lanes), f32)
-    after_x, inner, speed, ratio = pl.pallas_call(
+    )(pltpu.with_memory_space_constraint(c, pltpu.HBM))
+    first = lax.ppermute(first, "lines", neighbours(0, line_count))
+    second = lax.ppermute(second, "lines", neighbours(1, line_count))
+    ratio = jnp.full((rows, lanes), step_ratio)
+    after_x, inner, speed = pl.pallas_call(
         inner_kernel,
-        out_shape=[whole, whole, tile, tile],
-        in_specs=[hbm, vmem],
-        out_specs=[vmem] * 4,
-        scratch_shapes=[pltpu.SMEM((1, 1), f32), pltpu.SemaphoreType.DMA],
+        out_shape=[whole, whole, tile],
+        in_specs=[vmem] * 2,
+        out_specs=[vmem] * 3,
         compiler_params=params,
         cost_estimate=pl.CostEstimate(flops=20_000_000, bytes_accessed=1_400_000, transcendentals=500_000),
-    )(step_ratio.reshape(1, 1), own)
-    line = lax.axis_index("lines")
-    place = jnp.stack([line == 0, line == line_count - 1]).astype(jnp.int32).reshape(1, 2)
-    first_groups = groups_of(("z", "core"), {"z": 5})
-    second_groups = groups_of(("y_hi", "y_lo", "x"), {"y_hi": 2, "x": 2})
+    )(ratio, own)
+    first_groups = groups_of(('half', 'x', 'core'), {'half': 1, 'x': 2})
+    second_groups = groups_of(('depth', 'y_hi', 'y_lo'), {'depth': 2, 'y_hi': 2, 'y_lo': 0})
     advanced, top = pl.pallas_call(
-        outer_kernel,
+        functools.partial(outer_kernel, line_count),
         out_shape=[whole, jax.ShapeDtypeStruct((len(first_groups[0]), lanes), f32)],
-        in_specs=[smem] + [vmem] * 6,
+        in_specs=[vmem] * 6,
         out_specs=[anywhere, vmem],
         scratch_shapes=[
             pltpu.VMEM((fields, rows * rows, lanes), f32),
@@ -365,7 +378,7 @@
             pltpu.SemaphoreType.DMA((3,)),
         ],
         compiler_params=params,
-    )(place, ratio, below, above, after_x, inner, speed)
+    )(ratio, first, second, after_x, inner, speed)
     advanced = advanced.reshape(fields, groups, tiles, rows, lanes)
     top = jnp.max(gather_all(top, names, first_groups), axis=(0, 1))
     top = jnp.broadcast_to(top[None, :], (len(second_groups[0]), lanes))

time: 45.6 us -> 44.9 us (0.985)
  local copies, waits for them, and re-layouts: 1.09 us -> 0.02 us
  blocking collectives: 30.6 us -> 31.4 us
  starting transfers between devices: 5.24 us -> 4.61 us
    unnamed x2 -> x0, local copies, waits for them, and re-layouts: 1.08 us -> none
    pallas_call x1, Pallas kernels: 0.15 us -> 1.17 us  [body(): pl.pallas_call(load_kernel, out_shape=[whole, edge, edge], in_specs=[hbm]...]
    all_to_all x2, blocking collectives: 30.6 us -> 31.4 us  [gather_all(): lax.all_to_all(best[:, None, :], names, 0, 0, axis_index_groups=groups)]
    pallas_call x2, Pallas kernels: 5.68 us -> 4.95 us  [the longest x1 3.39 us: body(): pl.pallas_call(inner_kernel, out_shape=[whole, whole, tile], in_specs=[vm...]
    ppermute x2, starting transfers between devices: 5.24 us -> 4.61 us  [the longest x1 3.95 us: body(): first = lax.ppermute(first, 'lines', neighbours(0, line_count))]
where the time goes in v4:
time: 44.9 us; the launch traced here: 44.1 us
  blocking collectives  31.4 us (70%)
  Pallas kernels  6.12 us (14%)
  starting transfers between devices  4.61 us (10%)
  between operations  1.34 us (3%)
  other arithmetic  0.64 us (1%)
    all_to_all x2, blocking collectives, gather_all(): lax.all_to_all(best[:, None, :], names, 0, 0, axis_index_groups=groups)  31.4 us
    ppermute x1, starting transfers between devices, body(): first = lax.ppermute(first, 'lines', neighbours(0, line_count))  3.95 us
    pallas_call x1, Pallas kernels, body(): pl.pallas_call(inner_kernel, out_shape=[whole, whole, tile], in_specs=[vm...  3.39 us
    pallas_call x1, Pallas kernels, body(): pl.pallas_call(functools.partial(outer_kernel, line_count), out_shape=[wh...  1.56 us
    pallas_call x1, Pallas kernels, body(): pl.pallas_call(load_kernel, out_shape=[whole, edge, edge], in_specs=[hbm]...  1.17 us
  transfers between devices with their start and end apart: 2, of which 0 were waited for; matrix products, arithmetic and copies ran while one was open for 0% of the time, Pallas kernels for 8%

profile of v4, /device:TPU:1, one launch (start us, length us, event | category | flops | bytes accessed | tf_op | source)
XLA Modules:
  0.0 44.1 jit_solution(14166134205140836336)
XLA Ops:
  0.6 1.2 %shard_map.41 = (f32[5,256,128]{2,1,0:T(8,128)S(1)}, f32[5,24,128]{2,1,0:T(8,128)S(1)}, f32[5,24,128]{2,1,0:T(8,128)S(1)}) custom-call(f32[5,256,128]{2,1,0:T(8,128)} %bitcast.15), custom_call_target="tpu_custom_call" | custom-call | tf_op jit(solution)/shard_map/pallas_call | solution.py:349
  1.8 3.9 %collective-permute-start = (f32[5,24,128]{2,1,0:T(8,128)S(1)}, f32[5,24,128]{2,1,0:T(8,128)S(1)}, u32[]{:S(2)}, u32[]{:S(2)}) collective-permute-start(f32[5,24,128]{2,1,0:T(8,128)S(1)} %get-tuple-element.10), channel_id=1, source_target_pairs={{0,1},{1,0},{2,3},{3,2},{4,5},{5,4},{6,7},{7,6},{8,9},{9,8},{10,11... | collective-permute-start | bytes 184328 | tf_op jit(solution)/shard_map/ppermute | solution.py:357
  5.8 0.7 %collective-permute-start.1 = (f32[5,24,128]{2,1,0:T(8,128)S(1)}, f32[5,24,128]{2,1,0:T(8,128)S(1)}, u32[]{:S(2)}, u32[]{:S(2)}) collective-permute-start(f32[5,24,128]{2,1,0:T(8,128)S(1)} %get-tuple-element.11), channel_id=1, source_target_pairs={{1,2},{2,1},{3,4},{4,3},{5,6},{6,5},{9,10},{10,9},{11,12},{12,11},... | collective-permute-start | bytes 184328 | tf_op jit(solution)/shard_map/ppermute | solution.py:358
  7.1 3.4 %shard_map.42 = (f32[5,256,128]{2,1,0:T(8,128)S(1)}, f32[5,256,128]{2,1,0:T(8,128)S(1)}, f32[8,128]{1,0:T(8,128)S(1)}) custom-call(f32[8,128]{1,0:T(8,128)S(1)} %broadcast_in_dim.7.ratio_ref, f32[5,256,128]{2,1,0:T(8,128)S(1)} %get-tuple-element.12.c_ref), custom_call_target="tpu_custom_call" | custom-call | flops 20000000 | bytes 1400000 | tf_op jit(solution)/shard_map/pallas_call | solution.py:360
  10.5 0.0 collective-permute-done.first_ref
  10.5 0.0 collective-permute-done.1.second_ref
  10.5 1.6 %shard_map.43 = (f32[5,256,128]{2,1,0:T(8,128)}, f32[16,128]{1,0:T(8,128)S(1)}) custom-call(f32[8,128]{1,0:T(8,128)S(1)} %broadcast_in_dim.7.ratio_ref, f32[5,24,128]{2,1,0:T(8,128)S(1)} %collective-permute-done.first_ref, f32[5,24,128]{2,1,0:T(8,128)S(1)} %collective-permute-done.1.second_ref, f32[5,256,128]{2,1,0:T(8,128)S(1)} %get-tuple-element.13.ax_ref, ...), custom_call_target="tpu_custom_call" | custom-call | tf_op jit(solution)/shard_map/pallas_call | solution.py:370
  12.1 19.2 %all_to_all.10 = f32[16,1,128]{2,1,0:T(1,128)S(1)} all-to-all(f32[16,1,128]{2,1,0:T(1,128)S(1)} %bitcast.14), channel_id=1, replica_groups={{450,451,448,449,458,459,456,457,2,3,0,1,10,11,8,9},{454,455,452,453,46..., dimensions={0} | all-to-all | bytes 16384 | tf_op jit(solution)/shard_map/all_to_all | solution.py:330
  31.3 12.2 %all_to_all.11 = f32[32,1,128]{2,1,0:T(1,128)S(1)} all-to-all(f32[32,1,128]{2,1,0:T(1,128)S(1)} %broadcast_in_dim_broadcast_in_dim.2), channel_id=1, replica_groups={{160,164,176,180,128,132,144,148,224,228,240,244,192,196,208,212,32,36,..., dimensions={0} | all-to-all | bytes 32768 | tf_op jit(solution)/shard_map/all_to_all | solution.py:330
  43.5 0.6 %divide_reduce_fusion = f32[]{:T(128)} fusion(f32[32,1,128]{2,0,1:T(8,128)S(1)} %bitcast.16), kind=kLoop, calls=%fused_computation | loop fusion | flops 8191 | bytes 16388 | tf_op jit(solution)/shard_map/reduce_min | solution.py:385
  (3 shorter events, 0.1 us)
Async XLA Ops:
  1.8 8.7 %collective-permute-start = (f32[5,24,128]{2,1,0:T(8,128)S(1)}, f32[5,24,128]{2,1,0:T(8,128)S(1)}, u32[]{:S(2)}, u32[]{:S(2)}) collective-permute-start(f32[5,24,128]{2,1,0:T(8,128)S(1)} %get-tuple-element.10), channel_id=1, source_target_pairs={{0,1},{1,0},{2,3},{3,2},{4,5},{5,4},{6,7},{7,6},{8,9},{9,8},{10,11... | collective-permute-start | bytes 184328 | tf_op jit(solution)/shard_map/ppermute | solution.py:357
  5.8 4.7 %collective-permute-start.1 = (f32[5,24,128]{2,1,0:T(8,128)S(1)}, f32[5,24,128]{2,1,0:T(8,128)S(1)}, u32[]{:S(2)}, u32[]{:S(2)}) collective-permute-start(f32[5,24,128]{2,1,0:T(8,128)S(1)} %get-tuple-element.11), channel_id=1, source_target_pairs={{1,2},{2,1},{3,4},{4,3},{5,6},{6,5},{9,10},{10,9},{11,12},{12,11},... | collective-permute-start | bytes 184328 | tf_op jit(solution)/shard_map/ppermute | solution.py:358

commit v5 on v4

--- a/solution.py
+++ b/solution.py
@@ -184,36 +184,45 @@
 def load_kernel(c_ref, in_ref, first_ref, second_ref, sem):
     tiles, block = rows, rows * rows
     last = c_ref.shape[1] - block
-    spans = [pl.ds(0, block), pl.ds(last, block), pl.ds(block, last - block)]
     copies = [
-        pltpu.make_async_copy(c_ref.at[:, span, :], in_ref.at[:, span, :], sem.at[k])
-        for k, span in enumerate(spans)
+        pltpu.make_async_copy(
+            c_ref.at[:, pl.ds(side * last, block), :], in_ref.at[:, pl.ds(side * block, block), :], sem.at[side]
+        )
+        for side in range(2)
     ]
     for copy in copies:
         copy.start()
-    copies[0].wait()
-    copies[1].wait()
-    even = lax.axis_index("lines") % 2 == 0
+    for copy in copies:
+        copy.wait()
+    even = lax.axis_index("lines") % 2 == 1
     for f in range(fields):
         for r in range(ghosts):
             low = in_ref[f, pl.ds(r, tiles, stride=rows), :]
-            high = in_ref[f, pl.ds(last + rows - ghosts + r, tiles, stride=rows), :]
+            high = in_ref[f, pl.ds(block + rows - ghosts + r, tiles, stride=rows), :]
             first_ref[f, pl.ds(r * tiles, tiles), :] = jnp.where(even, high, low)
             second_ref[f, pl.ds(r * tiles, tiles), :] = jnp.where(even, low, high)
-    copies[2].wait()
-
-
-def inner_kernel(ratio_ref, c_ref, ax_ref, o_ref, speed_ref):
+
+
+def inner_kernel(ratio_ref, edge_ref, c_ref, ax_ref, o_ref, speed_ref, middle_ref, sem):
     tiles, block = rows, rows * rows
     count = c_ref.shape[1] // rows
+    last = c_ref.shape[1] - block
+    fetch = pltpu.make_async_copy(c_ref.at[:, pl.ds(block, last - block), :], middle_ref, sem)
+    fetch.start()
     ratio = ratio_ref[...]
 
-    def sweep(g, carry):
-        base = pl.multiple_of(g * block, block)
-        sweep_group(lambda f, t: c_ref[f, pl.ds(base + t * rows, rows), :], ax_ref, base, ratio)
-        return carry
-
-    lax.fori_loop(0, count // rows, sweep, 0)
+    def sweep(in_ref, stride, shift):
+        def one(g, carry):
+            base = pl.multiple_of(g * block, block)
+            to = pl.multiple_of(g * stride + shift, block)
+            sweep_group(lambda f, t: in_ref[f, pl.ds(base + t * rows, rows), :], ax_ref, to, ratio)
+            return carry
+
+        return one
+
+    lax.fori_loop(0, 2, sweep(edge_ref, last, 0), 0)
+    fetch.wait()
+    lax.fori_loop(0, count // rows - 2, sweep(middle_ref, block, block), 0)
 
     def row(r):
         return [ax_ref[f, row_at(r), :] for f in range(fields)]
@@ -261,7 +270,7 @@
         for t in range(tiles):
             halo_ref[f, pl.ds(t, rows, stride=tiles), :] = swept[f][t]
     place = lax.axis_index("lines")
-    even = place % 2 == 0
+    even = place % 2 == 1
     best = speed_ref[...]
     copies = [middle]
     for side in range(2):
@@ -346,25 +355,31 @@
     edge = jax.ShapeDtypeStruct((fields, ghosts * tiles, lanes), f32)
     params = pltpu.CompilerParams(vmem_limit_bytes=24 * 1024 * 1024)
     tile = jax.ShapeDtypeStruct((rows, lanes), f32)
-    own, first, second = pl.pallas_call(
+    block = tiles * rows
+    c = pltpu.with_memory_space_constraint(c, pltpu.HBM)
+    ends, first, second = pl.pallas_call(
         load_kernel,
-        out_shape=[whole, edge, edge],
+        out_shape=[jax.ShapeDtypeStruct((fields, 2 * block, lanes), f32), edge, edge],
         in_specs=[hbm],
         out_specs=[vmem] * 3,
-        scratch_shapes=[pltpu.SemaphoreType.DMA((3,))],
+        scratch_shapes=[pltpu.SemaphoreType.DMA((2,))],
         compiler_params=params,
-    )(pltpu.with_memory_space_constraint(c, pltpu.HBM))
-    first = lax.ppermute(first, "lines", neighbours(0, line_count))
-    second = lax.ppermute(second, "lines", neighbours(1, line_count))
+    )(c)
+    first = lax.ppermute(first, "lines", neighbours(1, line_count))
+    second = lax.ppermute(second, "lines", neighbours(0, line_count))
     ratio = jnp.full((rows, lanes), step_ratio)
     after_x, inner, speed = pl.pallas_call(
         inner_kernel,
         out_shape=[whole, whole, tile],
-        in_specs=[vmem] * 2,
+        in_specs=[vmem, vmem, hbm],
         out_specs=[vmem] * 3,
+        scratch_shapes=[
+            pltpu.VMEM((fields, (groups - 2) * block, lanes), f32),
+            pltpu.SemaphoreType.DMA,
+        ],
         compiler_params=params,
         cost_estimate=pl.CostEstimate(flops=20_000_000, bytes_accessed=1_400_000, transcendentals=500_000),
-    )(ratio, own)
+    )(ratio, ends, c)
     first_groups = groups_of(('half', 'x', 'core'), {'half': 1, 'x': 2})
     second_groups = groups_of(('depth', 'y_hi', 'y_lo'), {'depth': 2, 'y_hi': 2, 'y_lo': 0})
     advanced, top = pl.pallas_call(

time: 44.9 us -> 44.6 us (level)
  blocking collectives: 31.4 us -> 28.7 us
  starting transfers between devices: 4.61 us -> 7.07 us
    all_to_all x2, blocking collectives: 31.4 us -> 28.7 us  [gather_all(): lax.all_to_all(best[:, None, :], names, 0, 0, axis_index_groups=groups)]
    ppermute x2, starting transfers between devices: 4.61 us -> 7.07 us  [the longest x1 6.4 us: body(): second = lax.ppermute(second, 'lines', neighbours(0, line_count))]
where the time goes in v5:
time: 44.6 us; the launch traced here: 43.8 us
  blocking collectives  28.7 us (64%)
  starting transfers between devices  7.07 us (16%)
  Pallas kernels  6 us (13%)
  between operations  1.34 us (3%)
  other arithmetic  0.64 us (1%)
    all_to_all x2, blocking collectives, gather_all(): lax.all_to_all(best[:, None, :], names, 0, 0, axis_index_groups=groups)  28.7 us
    ppermute x1, starting transfers between devices, body(): second = lax.ppermute(second, 'lines', neighbours(0, line_count))  6.4 us
    pallas_call x1, Pallas kernels, body(): pl.pallas_call(inner_kernel, out_shape=[whole, whole, tile], in_specs=[vm...  3.41 us
    pallas_call x1, Pallas kernels, body(): pl.pallas_call(functools.partial(outer_kernel, line_count), out_shape=[wh...  1.56 us
    pallas_call x1, Pallas kernels, body(): pl.pallas_call(load_kernel, out_shape=[jax.ShapeDtypeStruct((fields, 2 *...  1.04 us
  transfers between devices with their start and end apart: 2, of which 0 were waited for; matrix products, arithmetic and copies ran while one was open for 0% of the time, Pallas kernels for 8%

profile of v5, /device:TPU:1, one launch (start us, length us, event | category | flops | bytes accessed | tf_op | source)
XLA Modules:
  0.0 43.8 jit_solution(688148080962506217)
XLA Ops:
  0.6 1.0 %shard_map.41 = (f32[5,128,128]{2,1,0:T(8,128)S(1)}, f32[5,24,128]{2,1,0:T(8,128)S(1)}, f32[5,24,128]{2,1,0:T(8,128)S(1)}) custom-call(f32[5,256,128]{2,1,0:T(8,128)} %bitcast.15), custom_call_target="tpu_custom_call" | custom-call | tf_op jit(solution)/shard_map/pallas_call | solution.py:360
  1.7 0.7 %collective-permute-start = (f32[5,24,128]{2,1,0:T(8,128)S(1)}, f32[5,24,128]{2,1,0:T(8,128)S(1)}, u32[]{:S(2)}, u32[]{:S(2)}) collective-permute-start(f32[5,24,128]{2,1,0:T(8,128)S(1)} %get-tuple-element.10), channel_id=1, source_target_pairs={{1,2},{2,1},{3,4},{4,3},{5,6},{6,5},{9,10},{10,9},{11,12},{12,11},... | collective-permute-start | bytes 184328 | tf_op jit(solution)/shard_map/ppermute | solution.py:368
  2.3 6.4 %collective-permute-start.1 = (f32[5,24,128]{2,1,0:T(8,128)S(1)}, f32[5,24,128]{2,1,0:T(8,128)S(1)}, u32[]{:S(2)}, u32[]{:S(2)}) collective-permute-start(f32[5,24,128]{2,1,0:T(8,128)S(1)} %get-tuple-element.11), channel_id=1, source_target_pairs={{0,1},{1,0},{2,3},{3,2},{4,5},{5,4},{6,7},{7,6},{8,9},{9,8},{10,11... | collective-permute-start | bytes 184328 | tf_op jit(solution)/shard_map/ppermute | solution.py:369
  9.4 3.4 %shard_map.42 = (f32[5,256,128]{2,1,0:T(8,128)S(1)}, f32[5,256,128]{2,1,0:T(8,128)S(1)}, f32[8,128]{1,0:T(8,128)S(1)}) custom-call(f32[8,128]{1,0:T(8,128)S(1)} %broadcast_in_dim.7.ratio_ref, f32[5,128,128]{2,1,0:T(8,128)S(1)} %get-tuple-element.12.edge_ref, f32[5,256,128]{2,1,0:T(8,128)} %bitcast.16), custom_call_target="tpu_custom_call" | custom-call | flops 20000000 | bytes 1400000 | tf_op jit(solution)/shard_map/pallas_call | solution.py:371
  12.8 0.0 collective-permute-done.first_ref
  12.8 0.0 collective-permute-done.1.second_ref
  12.9 1.6 %shard_map.43 = (f32[5,256,128]{2,1,0:T(8,128)}, f32[16,128]{1,0:T(8,128)S(1)}) custom-call(f32[8,128]{1,0:T(8,128)S(1)} %broadcast_in_dim.7.ratio_ref, f32[5,24,128]{2,1,0:T(8,128)S(1)} %collective-permute-done.first_ref, f32[5,24,128]{2,1,0:T(8,128)S(1)} %collective-permute-done.1.second_ref, f32[5,256,128]{2,1,0:T(8,128)S(1)} %get-tuple-element.13.ax_ref, ...), custom_call_target="tpu_custom_call" | custom-call | tf_op jit(solution)/shard_map/pallas_call | solution.py:385
  14.4 16.5 %all_to_all.10 = f32[16,1,128]{2,1,0:T(1,128)S(1)} all-to-all(f32[16,1,128]{2,1,0:T(1,128)S(1)} %bitcast.14), channel_id=1, replica_groups={{450,451,448,449,458,459,456,457,2,3,0,1,10,11,8,9},{454,455,452,453,46..., dimensions={0} | all-to-all | bytes 16384 | tf_op jit(solution)/shard_map/all_to_all | solution.py:339
  31.0 12.2 %all_to_all.11 = f32[32,1,128]{2,1,0:T(1,128)S(1)} all-to-all(f32[32,1,128]{2,1,0:T(1,128)S(1)} %broadcast_in_dim_broadcast_in_dim.2), channel_id=1, replica_groups={{160,164,176,180,128,132,144,148,224,228,240,244,192,196,208,212,32,36,..., dimensions={0} | all-to-all | bytes 32768 | tf_op jit(solution)/shard_map/all_to_all | solution.py:339
  43.1 0.6 %divide_reduce_fusion = f32[]{:T(128)} fusion(f32[32,1,128]{2,0,1:T(8,128)S(1)} %bitcast.17), kind=kLoop, calls=%fused_computation | loop fusion | flops 8191 | bytes 16388 | tf_op jit(solution)/shard_map/reduce_min | solution.py:400
  (3 shorter events, 0.1 us)
Async XLA Ops:
  1.7 11.2 %collective-permute-start = (f32[5,24,128]{2,1,0:T(8,128)S(1)}, f32[5,24,128]{2,1,0:T(8,128)S(1)}, u32[]{:S(2)}, u32[]{:S(2)}) collective-permute-start(f32[5,24,128]{2,1,0:T(8,128)S(1)} %get-tuple-element.10), channel_id=1, source_target_pairs={{1,2},{2,1},{3,4},{4,3},{5,6},{6,5},{9,10},{10,9},{11,12},{12,11},... | collective-permute-start | bytes 184328 | tf_op jit(solution)/shard_map/ppermute | solution.py:368
  2.3 10.5 %collective-permute-start.1 = (f32[5,24,128]{2,1,0:T(8,128)S(1)}, f32[5,24,128]{2,1,0:T(8,128)S(1)}, u32[]{:S(2)}, u32[]{:S(2)}) collective-permute-start(f32[5,24,128]{2,1,0:T(8,128)S(1)} %get-tuple-element.11), channel_id=1, source_target_pairs={{0,1},{1,0},{2,3},{3,2},{4,5},{5,4},{6,7},{7,6},{8,9},{9,8},{10,11... | collective-permute-start | bytes 184328 | tf_op jit(solution)/shard_map/ppermute | solution.py:369

commit v6 on v5

--- a/solution.py
+++ b/solution.py
@@ -250,15 +250,13 @@
 
 
 def outer_kernel(
-    line_count, ratio_ref, first_ref, second_ref, ax_ref, inner_ref, speed_ref, o_ref, top_ref, halo_ref, side_ref, sem
+    line_count, ratio_ref, first_ref, second_ref, ax_ref, inner_ref, speed_ref, o_ref, top_ref, halo_ref, new_ref, sem
 ):
     ratio = ratio_ref[...]
     tiles, block = rows, rows * rows
-    last = inner_ref.shape[1] - block
-    middle = pltpu.make_async_copy(
-        inner_ref.at[:, pl.ds(block, last - block), :], o_ref.at[:, pl.ds(block, last - block), :], sem.at[0]
-    )
-    middle.start()
+    groups = o_ref.shape[1]
+    whole = pltpu.make_async_copy(inner_ref, o_ref, sem.at[0])
+    whole.start()
     edge = ghosts * tiles
     for f in range(fields):
         halo_ref[f, pl.ds(0, edge), :] = first_ref[f]
@@ -272,10 +270,8 @@
     place = lax.axis_index("lines")
     even = place % 2 == 1
     best = speed_ref[...]
-    copies = [middle]
+    copies, news = [], []
     for side in range(2):
-        start = last if side else 0
-        side_ref[side] = inner_ref[:, pl.ds(start, block), :]
         first = ax_ref.shape[1] // tiles - 6 if side else 0
         inside = [
             [ax_ref[f, pl.ds((first + r) * rows, rows), :] for f in range(fields)] for r in range(6)
@@ -305,15 +301,21 @@
             new = march(state, line[r], lambda: line[r - ghosts], ratio)
             if new is None:
                 continue
-            p = r - 6 + (rows - ghosts if side else 0)
+            p = r - 6
             for f in range(fields):
-                side_ref[side, f, pl.ds(p, rows, stride=tiles), :] = new[f]
-            best = jnp.maximum(best, signal_speed(new))
-        copy = pltpu.make_async_copy(
-            side_ref.at[side], o_ref.at[:, pl.ds(start, block), :], sem.at[1 + side]
-        )
+                new_ref[side * ghosts + p, f] = new[f]
+            g, at = (groups - 1, rows - ghosts + p) if side else (0, p)
+            copies.append(
+                pltpu.make_async_copy(
+                    new_ref.at[side * ghosts + p], o_ref.at[:, g, :, at, :], sem.at[1 + side * ghosts + p]
+                )
+            )
+            news.append(new)
+    whole.wait()
+    for copy in copies:
         copy.start()
-        copies.append(copy)
+    for new in news:
+        best = jnp.maximum(best, signal_speed(new))
     best = jnp.max(ratio * best, axis=0, keepdims=True)
     top_ref[...] = jnp.broadcast_to(best, top_ref.shape)
     for copy in copies:
@@ -382,19 +384,19 @@
     )(ratio, ends, c)
     first_groups = groups_of(('half', 'x', 'core'), {'half': 1, 'x': 2})
     second_groups = groups_of(('depth', 'y_hi', 'y_lo'), {'depth': 2, 'y_hi': 2, 'y_lo': 0})
+    split = jax.ShapeDtypeStruct((fields, groups, tiles, rows, lanes), f32)
     advanced, top = pl.pallas_call(
         functools.partial(outer_kernel, line_count),
-        out_shape=[whole, jax.ShapeDtypeStruct((len(first_groups[0]), lanes), f32)],
+        out_shape=[split, jax.ShapeDtypeStruct((len(first_groups[0]), lanes), f32)],
         in_specs=[vmem] * 6,
         out_specs=[anywhere, vmem],
         scratch_shapes=[
             pltpu.VMEM((fields, rows * rows, lanes), f32),
-            pltpu.VMEM((2, fields, rows * rows, lanes), f32),
-            pltpu.SemaphoreType.DMA((3,)),
+            pltpu.VMEM((2 * ghosts, fields, tiles, lanes), f32),
+            pltpu.SemaphoreType.DMA((1 + 2 * ghosts,)),
         ],
         compiler_params=params,
-    )(ratio, first, second, after_x, inner, speed)
-    advanced = advanced.reshape(fields, groups, tiles, rows, lanes)
+    )(ratio, first, second, after_x, inner.reshape(split.shape), speed)
     top = jnp.max(gather_all(top, names, first_groups), axis=(0, 1))
     top = jnp.broadcast_to(top[None, :], (len(second_groups[0]), lanes))
     step_margin = jnp.min(safety / gather_all(top, names, second_groups))

time: 44.6 us -> 44.6 us (level)
  no operation moved by 1% of the time
where the time goes in v6:
time: 44.6 us; the launch traced here: 43.8 us
  blocking collectives  28.7 us (64%)
  starting transfers between devices  7.07 us (16%)
  Pallas kernels  6 us (13%)
  between operations  1.34 us (3%)
  other arithmetic  0.64 us (1%)
    all_to_all x2, blocking collectives, gather_all(): lax.all_to_all(best[:, None, :], names, 0, 0, axis_index_groups=groups)  28.7 us
    ppermute x1, starting transfers between devices, body(): second = lax.ppermute(second, 'lines', neighbours(0, line_count))  6.4 us
    pallas_call x1, Pallas kernels, body(): pl.pallas_call(inner_kernel, out_shape=[whole, whole, tile], in_specs=[vm...  3.41 us
    pallas_call x1, Pallas kernels, body(): pl.pallas_call(functools.partial(outer_kernel, line_count), out_shape=[sp...  1.56 us
    pallas_call x1, Pallas kernels, body(): pl.pallas_call(load_kernel, out_shape=[jax.ShapeDtypeStruct((fields, 2 *...  1.04 us
  transfers between devices with their start and end apart: 2, of which 0 were waited for; matrix products, arithmetic and copies ran while one was open for 0% of the time, Pallas kernels for 8%

profile of v6, /device:TPU:1, one launch (start us, length us, event | category | flops | bytes accessed | tf_op | source)
XLA Modules:
  0.0 43.8 jit_solution(8205841775097687960)
XLA Ops:
  0.6 1.0 %shard_map.41 = (f32[5,128,128]{2,1,0:T(8,128)S(1)}, f32[5,24,128]{2,1,0:T(8,128)S(1)}, f32[5,24,128]{2,1,0:T(8,128)S(1)}) custom-call(f32[5,256,128]{2,1,0:T(8,128)} %bitcast.15), custom_call_target="tpu_custom_call" | custom-call | tf_op jit(solution)/shard_map/pallas_call | solution.py:362
  1.7 0.7 %collective-permute-start = (f32[5,24,128]{2,1,0:T(8,128)S(1)}, f32[5,24,128]{2,1,0:T(8,128)S(1)}, u32[]{:S(2)}, u32[]{:S(2)}) collective-permute-start(f32[5,24,128]{2,1,0:T(8,128)S(1)} %get-tuple-element.10), channel_id=1, source_target_pairs={{1,2},{2,1},{3,4},{4,3},{5,6},{6,5},{9,10},{10,9},{11,12},{12,11},... | collective-permute-start | bytes 184328 | tf_op jit(solution)/shard_map/ppermute | solution.py:370
  2.3 6.4 %collective-permute-start.1 = (f32[5,24,128]{2,1,0:T(8,128)S(1)}, f32[5,24,128]{2,1,0:T(8,128)S(1)}, u32[]{:S(2)}, u32[]{:S(2)}) collective-permute-start(f32[5,24,128]{2,1,0:T(8,128)S(1)} %get-tuple-element.11), channel_id=1, source_target_pairs={{0,1},{1,0},{2,3},{3,2},{4,5},{5,4},{6,7},{7,6},{8,9},{9,8},{10,11... | collective-permute-start | bytes 184328 | tf_op jit(solution)/shard_map/ppermute | solution.py:371
  9.4 3.4 %shard_map.42 = (f32[5,256,128]{2,1,0:T(8,128)S(1)}, f32[5,256,128]{2,1,0:T(8,128)S(1)}, f32[8,128]{1,0:T(8,128)S(1)}) custom-call(f32[8,128]{1,0:T(8,128)S(1)} %broadcast_in_dim.7.ratio_ref, f32[5,128,128]{2,1,0:T(8,128)S(1)} %get-tuple-element.12.edge_ref, f32[5,256,128]{2,1,0:T(8,128)} %bitcast.16), custom_call_target="tpu_custom_call" | custom-call | flops 20000000 | bytes 1400000 | tf_op jit(solution)/shard_map/pallas_call | solution.py:373
  12.8 0.0 collective-permute-done.first_ref
  12.8 0.0 collective-permute-done.1.second_ref
  12.9 1.6 %shard_map.43 = (f32[5,4,8,8,128]{4,3,2,1,0:T(8,128)}, f32[16,128]{1,0:T(8,128)S(1)}) custom-call(f32[8,128]{1,0:T(8,128)S(1)} %broadcast_in_dim.7.ratio_ref, f32[5,24,128]{2,1,0:T(8,128)S(1)} %collective-permute-done.first_ref, f32[5,24,128]{2,1,0:T(8,128)S(1)} %collective-permute-done.1.second_ref, f32[5,256,128]{2,1,0:T(8,128)S(1)} %get-tuple-element.13.ax_ref, ...), custom_call_target="tpu_custom_call" | custom-call | tf_op jit(solution)/shard_map/pallas_call | solution.py:388
  14.4 16.5 %all_to_all.10 = f32[16,1,128]{2,1,0:T(1,128)S(1)} all-to-all(f32[16,1,128]{2,1,0:T(1,128)S(1)} %bitcast.14), channel_id=1, replica_groups={{450,451,448,449,458,459,456,457,2,3,0,1,10,11,8,9},{454,455,452,453,46..., dimensions={0} | all-to-all | bytes 16384 | tf_op jit(solution)/shard_map/all_to_all | solution.py:341
  31.0 12.2 %all_to_all.11 = f32[32,1,128]{2,1,0:T(1,128)S(1)} all-to-all(f32[32,1,128]{2,1,0:T(1,128)S(1)} %broadcast_in_dim_broadcast_in_dim.2), channel_id=1, replica_groups={{160,164,176,180,128,132,144,148,224,228,240,244,192,196,208,212,32,36,..., dimensions={0} | all-to-all | bytes 32768 | tf_op jit(solution)/shard_map/all_to_all | solution.py:341
  43.1 0.6 %divide_reduce_fusion = f32[]{:T(128)} fusion(f32[32,1,128]{2,0,1:T(8,128)S(1)} %bitcast.17), kind=kLoop, calls=%fused_computation | loop fusion | flops 8191 | bytes 16388 | tf_op jit(solution)/shard_map/reduce_min | solution.py:402
  (3 shorter events, 0.1 us)
Async XLA Ops:
  1.7 11.2 %collective-permute-start = (f32[5,24,128]{2,1,0:T(8,128)S(1)}, f32[5,24,128]{2,1,0:T(8,128)S(1)}, u32[]{:S(2)}, u32[]{:S(2)}) collective-permute-start(f32[5,24,128]{2,1,0:T(8,128)S(1)} %get-tuple-element.10), channel_id=1, source_target_pairs={{1,2},{2,1},{3,4},{4,3},{5,6},{6,5},{9,10},{10,9},{11,12},{12,11},... | collective-permute-start | bytes 184328 | tf_op jit(solution)/shard_map/ppermute | solution.py:370
  2.3 10.5 %collective-permute-start.1 = (f32[5,24,128]{2,1,0:T(8,128)S(1)}, f32[5,24,128]{2,1,0:T(8,128)S(1)}, u32[]{:S(2)}, u32[]{:S(2)}) collective-permute-start(f32[5,24,128]{2,1,0:T(8,128)S(1)} %get-tuple-element.11), channel_id=1, source_target_pairs={{0,1},{1,0},{2,3},{3,2},{4,5},{5,4},{6,7},{7,6},{8,9},{9,8},{10,11... | collective-permute-start | bytes 184328 | tf_op jit(solution)/shard_map/ppermute | solution.py:371

commit v7 on v6

--- a/solution.py
+++ b/solution.py
@@ -36,9 +36,8 @@
     return jnp.maximum(jnp.minimum(offset, bound), jnp.minimum(jnp.maximum(offset, bound), 0.0))
 
 
-def half_state(state, normal):
-    density, pressure = state[0], state[4]
-    ratio = pressure * (1.0 / density)
+def half_state(state, inverse, normal):
+    ratio = state[4] * inverse
     sound = jnp.sqrt(adiabatic * ratio)
     kinetic = state[1] * state[1] + state[2] * state[2] + state[3] * state[3]
     specific = 1.0 / (adiabatic - 1.0) * ratio + 0.5 * kinetic
@@ -46,8 +45,9 @@
 
 
 def hll_flux(left, right, normal):
-    ul, cl, el = half_state(left, normal)
-    ur, cr, er = half_state(right, normal)
+    both = 1.0 / (left[0] * right[0])
+    ul, cl, el = half_state(left, right[0] * both, normal)
+    ur, cr, er = half_state(right, left[0] * both, normal)
     slowest = jnp.minimum(jnp.minimum(ul - cl, ur - cr), 0.0)
     fastest = jnp.maximum(jnp.maximum(ul + cl, ur + cr), 0.0)
     inverse = 1.0 / (fastest - slowest)

time: 44.6 us -> 44.6 us (level)
  no operation moved by 1% of the time
where the time goes in v7:
time: 44.6 us; the launch traced here: 43.8 us
  blocking collectives  28.7 us (64%)
  starting transfers between devices  7.07 us (16%)
  Pallas kernels  6.03 us (14%)
  between operations  1.34 us (3%)
  other arithmetic  0.64 us (1%)
    all_to_all x2, blocking collectives, gather_all(): lax.all_to_all(best[:, None, :], names, 0, 0, axis_index_groups=groups)  28.7 us
    ppermute x1, starting transfers between devices, body(): second = lax.ppermute(second, 'lines', neighbours(0, line_count))  6.4 us
    pallas_call x1, Pallas kernels, body(): pl.pallas_call(inner_kernel, out_shape=[whole, whole, tile], in_specs=[vm...  3.44 us
    pallas_call x1, Pallas kernels, body(): pl.pallas_call(functools.partial(outer_kernel, line_count), out_shape=[sp...  1.56 us
    pallas_call x1, Pallas kernels, body(): pl.pallas_call(load_kernel, out_shape=[jax.ShapeDtypeStruct((fields, 2 *...  1.04 us
  transfers between devices with their start and end apart: 2, of which 0 were waited for; matrix products, arithmetic and copies ran while one was open for 0% of the time, Pallas kernels for 8%

profile of v7, /device:TPU:1, one launch (start us, length us, event | category | flops | bytes accessed | tf_op | source)
XLA Modules:
  0.0 43.8 jit_solution(17350445904156679711)
XLA Ops:
  0.6 1.0 %shard_map.41 = (f32[5,128,128]{2,1,0:T(8,128)S(1)}, f32[5,24,128]{2,1,0:T(8,128)S(1)}, f32[5,24,128]{2,1,0:T(8,128)S(1)}) custom-call(f32[5,256,128]{2,1,0:T(8,128)} %bitcast.15), custom_call_target="tpu_custom_call" | custom-call | tf_op jit(solution)/shard_map/pallas_call | solution.py:362
  1.7 0.7 %collective-permute-start = (f32[5,24,128]{2,1,0:T(8,128)S(1)}, f32[5,24,128]{2,1,0:T(8,128)S(1)}, u32[]{:S(2)}, u32[]{:S(2)}) collective-permute-start(f32[5,24,128]{2,1,0:T(8,128)S(1)} %get-tuple-element.10), channel_id=1, source_target_pairs={{1,2},{2,1},{3,4},{4,3},{5,6},{6,5},{9,10},{10,9},{11,12},{12,11},... | collective-permute-start | bytes 184328 | tf_op jit(solution)/shard_map/ppermute | solution.py:370
  2.3 6.4 %collective-permute-start.1 = (f32[5,24,128]{2,1,0:T(8,128)S(1)}, f32[5,24,128]{2,1,0:T(8,128)S(1)}, u32[]{:S(2)}, u32[]{:S(2)}) collective-permute-start(f32[5,24,128]{2,1,0:T(8,128)S(1)} %get-tuple-element.11), channel_id=1, source_target_pairs={{0,1},{1,0},{2,3},{3,2},{4,5},{5,4},{6,7},{7,6},{8,9},{9,8},{10,11... | collective-permute-start | bytes 184328 | tf_op jit(solution)/shard_map/ppermute | solution.py:371
  9.4 3.4 %shard_map.42 = (f32[5,256,128]{2,1,0:T(8,128)S(1)}, f32[5,256,128]{2,1,0:T(8,128)S(1)}, f32[8,128]{1,0:T(8,128)S(1)}) custom-call(f32[8,128]{1,0:T(8,128)S(1)} %broadcast_in_dim.7.ratio_ref, f32[5,128,128]{2,1,0:T(8,128)S(1)} %get-tuple-element.12.edge_ref, f32[5,256,128]{2,1,0:T(8,128)} %bitcast.16), custom_call_target="tpu_custom_call" | custom-call | flops 20000000 | bytes 1400000 | tf_op jit(solution)/shard_map/pallas_call | solution.py:373
  12.9 0.0 collective-permute-done.first_ref
  12.9 0.0 collective-permute-done.1.second_ref
  12.9 1.6 %shard_map.43 = (f32[5,4,8,8,128]{4,3,2,1,0:T(8,128)}, f32[16,128]{1,0:T(8,128)S(1)}) custom-call(f32[8,128]{1,0:T(8,128)S(1)} %broadcast_in_dim.7.ratio_ref, f32[5,24,128]{2,1,0:T(8,128)S(1)} %collective-permute-done.first_ref, f32[5,24,128]{2,1,0:T(8,128)S(1)} %collective-permute-done.1.second_ref, f32[5,256,128]{2,1,0:T(8,128)S(1)} %get-tuple-element.13.ax_ref, ...), custom_call_target="tpu_custom_call" | custom-call | tf_op jit(solution)/shard_map/pallas_call | solution.py:388
  14.4 16.5 %all_to_all.10 = f32[16,1,128]{2,1,0:T(1,128)S(1)} all-to-all(f32[16,1,128]{2,1,0:T(1,128)S(1)} %bitcast.14), channel_id=1, replica_groups={{450,451,448,449,458,459,456,457,2,3,0,1,10,11,8,9},{454,455,452,453,46..., dimensions={0} | all-to-all | bytes 16384 | tf_op jit(solution)/shard_map/all_to_all | solution.py:341
  31.0 12.2 %all_to_all.11 = f32[32,1,128]{2,1,0:T(1,128)S(1)} all-to-all(f32[32,1,128]{2,1,0:T(1,128)S(1)} %broadcast_in_dim_broadcast_in_dim.2), channel_id=1, replica_groups={{160,164,176,180,128,132,144,148,224,228,240,244,192,196,208,212,32,36,..., dimensions={0} | all-to-all | bytes 32768 | tf_op jit(solution)/shard_map/all_to_all | solution.py:341
  43.2 0.6 %divide_reduce_fusion = f32[]{:T(128)} fusion(f32[32,1,128]{2,0,1:T(8,128)S(1)} %bitcast.17), kind=kLoop, calls=%fused_computation | loop fusion | flops 8191 | bytes 16388 | tf_op jit(solution)/shard_map/reduce_min | solution.py:402
  (3 shorter events, 0.1 us)
Async XLA Ops:
  1.7 11.2 %collective-permute-start = (f32[5,24,128]{2,1,0:T(8,128)S(1)}, f32[5,24,128]{2,1,0:T(8,128)S(1)}, u32[]{:S(2)}, u32[]{:S(2)}) collective-permute-start(f32[5,24,128]{2,1,0:T(8,128)S(1)} %get-tuple-element.10), channel_id=1, source_target_pairs={{1,2},{2,1},{3,4},{4,3},{5,6},{6,5},{9,10},{10,9},{11,12},{12,11},... | collective-permute-start | bytes 184328 | tf_op jit(solution)/shard_map/ppermute | solution.py:370
  2.3 10.5 %collective-permute-start.1 = (f32[5,24,128]{2,1,0:T(8,128)S(1)}, f32[5,24,128]{2,1,0:T(8,128)S(1)}, u32[]{:S(2)}, u32[]{:S(2)}) collective-permute-start(f32[5,24,128]{2,1,0:T(8,128)S(1)} %get-tuple-element.11), channel_id=1, source_target_pairs={{0,1},{1,0},{2,3},{3,2},{4,5},{5,4},{6,7},{7,6},{8,9},{9,8},{10,11... | collective-permute-start | bytes 184328 | tf_op jit(solution)/shard_map/ppermute | solution.py:371

commit v8 on v6

--- a/solution.py
+++ b/solution.py
@@ -194,13 +194,13 @@
         copy.start()
     for copy in copies:
         copy.wait()
-    even = lax.axis_index("lines") % 2 == 1
+    upward = (lax.axis_index("planes") + lax.axis_index("lines")) % 2 == 1
     for f in range(fields):
         for r in range(ghosts):
             low = in_ref[f, pl.ds(r, tiles, stride=rows), :]
             high = in_ref[f, pl.ds(block + rows - ghosts + r, tiles, stride=rows), :]
-            first_ref[f, pl.ds(r * tiles, tiles), :] = jnp.where(even, high, low)
-            second_ref[f, pl.ds(r * tiles, tiles), :] = jnp.where(even, low, high)
+            first_ref[f, pl.ds(r * tiles, tiles), :] = jnp.where(upward, high, low)
+            second_ref[f, pl.ds(r * tiles, tiles), :] = jnp.where(upward, low, high)
 
 
 def inner_kernel(ratio_ref, edge_ref, c_ref, ax_ref, o_ref, speed_ref, middle_ref, sem):
@@ -268,7 +268,7 @@
         for t in range(tiles):
             halo_ref[f, pl.ds(t, rows, stride=tiles), :] = swept[f][t]
     place = lax.axis_index("lines")
-    even = place % 2 == 1
+    upward = (lax.axis_index("planes") + place) % 2 == 1
     best = speed_ref[...]
     copies, news = [], []
     for side in range(2):
@@ -278,7 +278,7 @@
         ]
         end = inside[5] if side else inside[0]
         at_end = place == (line_count - 1 if side else 0)
-        from_first = even if side else jnp.logical_not(even)
+        from_first = upward if side else jnp.logical_not(upward)
         outside = [
             [
                 jnp.where(
@@ -333,8 +333,13 @@
     return numbers.transpose(order).reshape(-1, count).tolist()
 
 
-def neighbours(start, count):
-    return [p for i in range(start, count - 1, 2) for p in ((i, i + 1), (i + 1, i))]
+def neighbours(start, planes, lines):
+    pairs = []
+    for p in range(planes):
+        for i in range((start + p) % 2, lines - 1, 2):
+            here = p * lines + i
+            pairs += [(here, here + 1), (here + 1, here)]
+    return pairs
 
 
 def gather_all(best, names, groups):
@@ -367,8 +372,8 @@
         scratch_shapes=[pltpu.SemaphoreType.DMA((2,))],
         compiler_params=params,
     )(c)
-    first = lax.ppermute(first, "lines", neighbours(1, line_count))
-    second = lax.ppermute(second, "lines", neighbours(0, line_count))
+    first = lax.ppermute(first, names, neighbours(1, plane_count, line_count))
+    second = lax.ppermute(second, names, neighbours(0, plane_count, line_count))
     ratio = jnp.full((rows, lanes), step_ratio)
     after_x, inner, speed = pl.pallas_call(
         inner_kernel,

time: 44.6 us -> 44.6 us (level)
  starting transfers between devices: 7.07 us -> 4.61 us
  blocking collectives: 28.7 us -> 31.1 us
    ppermute x2, starting transfers between devices: 7.07 us -> 4.61 us  [the longest x1 3.95 us: body(): first = lax.ppermute(first, names, neighbours(1, plane_count, line_count))]
    all_to_all x2, blocking collectives: 28.7 us -> 31.1 us  [gather_all(): lax.all_to_all(best[:, None, :], names, 0, 0, axis_index_groups=groups)]
where the time goes in v8:
time: 44.6 us; the launch traced here: 43.7 us
  blocking collectives  31.1 us (70%)
  Pallas kernels  6 us (13%)
  starting transfers between devices  4.61 us (10%)
  between operations  1.34 us (3%)
  other arithmetic  0.64 us (1%)
    all_to_all x2, blocking collectives, gather_all(): lax.all_to_all(best[:, None, :], names, 0, 0, axis_index_groups=groups)  31.1 us
    ppermute x1, starting transfers between devices, body(): first = lax.ppermute(first, names, neighbours(1, plane_count, line_count))  3.95 us
    pallas_call x1, Pallas kernels, body(): pl.pallas_call(inner_kernel, out_shape=[whole, whole, tile], in_specs=[vm...  3.41 us
    pallas_call x1, Pallas kernels, body(): pl.pallas_call(functools.partial(outer_kernel, line_count), out_shape=[sp...  1.55 us
    pallas_call x1, Pallas kernels, body(): pl.pallas_call(load_kernel, out_shape=[jax.ShapeDtypeStruct((fields, 2 *...  1.04 us
  transfers between devices with their start and end apart: 2, of which 0 were waited for; matrix products, arithmetic and copies ran while one was open for 0% of the time, Pallas kernels for 8%

profile of v8, /device:TPU:1, one launch (start us, length us, event | category | flops | bytes accessed | tf_op | source)
XLA Modules:
  0.0 43.7 jit_solution(9730081261702220588)
XLA Ops:
  0.6 1.0 %shard_map.41 = (f32[5,128,128]{2,1,0:T(8,128)S(1)}, f32[5,24,128]{2,1,0:T(8,128)S(1)}, f32[5,24,128]{2,1,0:T(8,128)S(1)}) custom-call(f32[5,256,128]{2,1,0:T(8,128)} %bitcast.15), custom_call_target="tpu_custom_call" | custom-call | tf_op jit(solution)/shard_map/pallas_call | solution.py:367
  1.7 3.9 %collective-permute-start = (f32[5,24,128]{2,1,0:T(8,128)S(1)}, f32[5,24,128]{2,1,0:T(8,128)S(1)}, u32[]{:S(2)}, u32[]{:S(2)}) collective-permute-start(f32[5,24,128]{2,1,0:T(8,128)S(1)} %get-tuple-element.10), channel_id=1, source_target_pairs={{1,2},{2,1},{3,4},{4,3},{5,6},{6,5},{8,9},{9,8},{10,11},{11,10},{1... | collective-permute-start | bytes 184328 | tf_op jit(solution)/shard_map/ppermute | solution.py:375
  5.6 0.7 %collective-permute-start.1 = (f32[5,24,128]{2,1,0:T(8,128)S(1)}, f32[5,24,128]{2,1,0:T(8,128)S(1)}, u32[]{:S(2)}, u32[]{:S(2)}) collective-permute-start(f32[5,24,128]{2,1,0:T(8,128)S(1)} %get-tuple-element.11), channel_id=1, source_target_pairs={{0,1},{1,0},{2,3},{3,2},{4,5},{5,4},{6,7},{7,6},{9,10},{10,9},{11,... | collective-permute-start | bytes 184328 | tf_op jit(solution)/shard_map/ppermute | solution.py:376
  7.0 3.4 %shard_map.42 = (f32[5,256,128]{2,1,0:T(8,128)S(1)}, f32[5,256,128]{2,1,0:T(8,128)S(1)}, f32[8,128]{1,0:T(8,128)S(1)}) custom-call(f32[8,128]{1,0:T(8,128)S(1)} %broadcast_in_dim.7.ratio_ref, f32[5,128,128]{2,1,0:T(8,128)S(1)} %get-tuple-element.12.edge_ref, f32[5,256,128]{2,1,0:T(8,128)} %bitcast.16), custom_call_target="tpu_custom_call" | custom-call | flops 20000000 | bytes 1400000 | tf_op jit(solution)/shard_map/pallas_call | solution.py:378
  10.4 0.0 collective-permute-done.first_ref
  10.4 0.0 collective-permute-done.1.second_ref
  10.4 1.6 %shard_map.43 = (f32[5,4,8,8,128]{4,3,2,1,0:T(8,128)}, f32[16,128]{1,0:T(8,128)S(1)}) custom-call(f32[8,128]{1,0:T(8,128)S(1)} %broadcast_in_dim.7.ratio_ref, f32[5,24,128]{2,1,0:T(8,128)S(1)} %collective-permute-done.first_ref, f32[5,24,128]{2,1,0:T(8,128)S(1)} %collective-permute-done.1.second_ref, f32[5,256,128]{2,1,0:T(8,128)S(1)} %get-tuple-element.13.ax_ref, ...), custom_call_target="tpu_custom_call" | custom-call | tf_op jit(solution)/shard_map/pallas_call | solution.py:393
  12.0 19.0 %all_to_all.10 = f32[16,1,128]{2,1,0:T(1,128)S(1)} all-to-all(f32[16,1,128]{2,1,0:T(1,128)S(1)} %bitcast.14), channel_id=1, replica_groups={{450,451,448,449,458,459,456,457,2,3,0,1,10,11,8,9},{454,455,452,453,46..., dimensions={0} | all-to-all | bytes 16384 | tf_op jit(solution)/shard_map/all_to_all | solution.py:346
  31.0 12.2 %all_to_all.11 = f32[32,1,128]{2,1,0:T(1,128)S(1)} all-to-all(f32[32,1,128]{2,1,0:T(1,128)S(1)} %broadcast_in_dim_broadcast_in_dim.2), channel_id=1, replica_groups={{160,164,176,180,128,132,144,148,224,228,240,244,192,196,208,212,32,36,..., dimensions={0} | all-to-all | bytes 32768 | tf_op jit(solution)/shard_map/all_to_all | solution.py:346
  43.1 0.6 %divide_reduce_fusion = f32[]{:T(128)} fusion(f32[32,1,128]{2,0,1:T(8,128)S(1)} %bitcast.17), kind=kLoop, calls=%fused_computation | loop fusion | flops 8191 | bytes 16388 | tf_op jit(solution)/shard_map/reduce_min | solution.py:407
  (3 shorter events, 0.1 us)
Async XLA Ops:
  1.7 8.7 %collective-permute-start = (f32[5,24,128]{2,1,0:T(8,128)S(1)}, f32[5,24,128]{2,1,0:T(8,128)S(1)}, u32[]{:S(2)}, u32[]{:S(2)}) collective-permute-start(f32[5,24,128]{2,1,0:T(8,128)S(1)} %get-tuple-element.10), channel_id=1, source_target_pairs={{1,2},{2,1},{3,4},{4,3},{5,6},{6,5},{8,9},{9,8},{10,11},{11,10},{1... | collective-permute-start | bytes 184328 | tf_op jit(solution)/shard_map/ppermute | solution.py:375
  5.6 4.8 %collective-permute-start.1 = (f32[5,24,128]{2,1,0:T(8,128)S(1)}, f32[5,24,128]{2,1,0:T(8,128)S(1)}, u32[]{:S(2)}, u32[]{:S(2)}) collective-permute-start(f32[5,24,128]{2,1,0:T(8,128)S(1)} %get-tuple-element.11), channel_id=1, source_target_pairs={{0,1},{1,0},{2,3},{3,2},{4,5},{5,4},{6,7},{7,6},{9,10},{10,9},{11,... | collective-permute-start | bytes 184328 | tf_op jit(solution)/shard_map/ppermute | solution.py:376
